TPU v7x, 32 devices: a whole 2x2x4 slice. The times are simulated.
32 devices in a mesh: leaf: 8 (over z, x), front: 4 (over y, core).
Axes of the slice: x: 2, y: 2, z: 4, core: 2. Of those that a mesh axis runs over, the one named last changes fastest.
Arguments:
- leaf_update: float32 [8192, 1024], P('leaf'), as said below
- separator_rows_1: float32 [2048, 1536], P(('leaf', 'front')), as said below
- remaining_rows_1: float32 [4096, 1536], P(('leaf', 'front'))
- separator_rows_2: float32 [1024, 1536], P(('leaf', 'front')), as said below
- remaining_rows_2: float32 [2048, 1536], P(('leaf', 'front'))
- separator_rows_3: float32 [512, 1536], P(('leaf', 'front')), as said below
- remaining_rows_3: float32 [1024, 1536], P(('leaf', 'front'))
- child_map_1: int32 [8, 8], replicated, may hold values from 0 to 11, as said below
- child_map_2: int32 [4, 8], replicated, may hold values from 0 to 11, as said below
- child_map_3: int32 [2, 8], replicated, may hold values from 0 to 11, as said below
Outputs:
- pivot_factor_1: float32 [2048, 512], P(('leaf', 'front'))
- below_factor_1: float32 [4096, 512], P(('leaf', 'front'))
- pivot_factor_2: float32 [1024, 512], P(('leaf', 'front'))
- below_factor_2: float32 [2048, 512], P(('leaf', 'front'))
- pivot_factor_3: float32 [512, 512], P(('leaf', 'front'))
- below_factor_3: float32 [1024, 512], P(('leaf', 'front'))
Inputs may be any that keep to these rules, and one draw needn't show every extreme that they name: `child_map_1`: each row lists 8 distinct parent tiles in increasing order, the last one always 12 - 1. `child_map_2`: each row lists 8 distinct parent tiles in increasing order, the last one always 12 - 1. `child_map_3`: each row lists 8 distinct parent tiles in increasing order, the last one always 12 - 1. `leaf_update`: each block is symmetric positive definite, diagonal between 0.5 and 2, off-diagonal entries of magnitude about 0.008, smallest eigenvalue about 0.1 or more. Each front, separator_rows_1 above remaining_rows_1, is symmetric positive definite, diagonal between 2 and 4, off-diagonal entries of magnitude about 0.03, smallest eigenvalue about 0.35 or more. Each front, separator_rows_2 above remaining_rows_2, is symmetric positive definite, diagonal between 2 and 4, off-diagonal entries of magnitude about 0.03, smallest eigenvalue about 0.35 or more. Each front, separator_rows_3 above remaining_rows_3, is symmetric positive definite, diagonal between 2 and 4, off-diagonal entries of magnitude about 0.03, smallest eigenvalue about 0.35 or more.
All inputs are finite; a program needn't handle non-finite values.
Results may differ from a plain program's by a relative error of at most 0.0003.
Values sent between devices are 32-bit elements; how exact they have to be, the bound alone decides.
A program may use at most 128 MiB of HBM per device.

v0:
```python
import jax
import jax.numpy as jnp
from jax import lax
from jax.sharding import PartitionSpec as P

TILE = 128
SEP = 512
UPD = 1024
NF = 1536
NT = 12
UT = 8


def from_partner(block, axis, stride):
    count = lax.axis_size(axis)
    route = []
    for low in range(count):
        high = low | 1 << stride
        if high != low and high < count:
            route += [(low, high), (high, low)]
    return lax.ppermute(block, axis, route)


def collect(pieces, depth_count):
    gathered = lax.all_gather(pieces, "front", axis=0, tiled=True)
    leaf_place = lax.axis_index("leaf")
    for bit_number in range(depth_count):
        partner = from_partner(gathered, "leaf", bit_number)
        on_high = leaf_place >> bit_number & 1 == 1
        gathered = jnp.where(
            on_high,
            jnp.concatenate([partner, gathered], axis=0),
            jnp.concatenate([gathered, partner], axis=0),
        )
    return gathered


def owned_rows(position, group_count):
    sep_count = SEP // group_count
    upd_count = UPD // group_count
    sep_index = position * sep_count + jnp.arange(sep_count, dtype=jnp.int32)
    upd_index = SEP + position * upd_count + jnp.arange(upd_count, dtype=jnp.int32)
    return jnp.concatenate([sep_index, upd_index])


def locate(tile_map, targets):
    tile_of = targets // TILE
    offset = targets % TILE
    matches = tile_map[None, :] == tile_of[:, None]
    present = jnp.any(matches, axis=1)
    slot_ids = jnp.arange(tile_map.shape[0], dtype=jnp.int32)
    source = jnp.sum(jnp.where(matches, slot_ids[None, :], 0), axis=1)
    return (source * TILE + offset, present)


def select_rows(full_update, tile_map, targets):
    source, present = locate(tile_map, targets)
    return jnp.where(present[:, None], jnp.take(full_update, source, axis=0), 0.0)


def expand_columns(row_block, tile_map):
    placing = (tile_map[:, None] == jnp.arange(NT, dtype=jnp.int32)[None, :]).astype(jnp.float32)
    tiled = row_block.reshape(row_block.shape[0], UT, TILE)
    placed = jnp.einsum("rut,un->rnt", tiled, placing, precision=lax.Precision.HIGHEST)
    return placed.reshape(row_block.shape[0], NF)


def body(
    leaf_update,
    separator_rows_1,
    remaining_rows_1,
    separator_rows_2,
    remaining_rows_2,
    separator_rows_3,
    remaining_rows_3,
    child_map_1,
    child_map_2,
    child_map_3,
):
    leaf_place = lax.axis_index("leaf")
    front_place = lax.axis_index("front")
    front_count = lax.axis_size("front")
    child_full = leaf_update
    sections = (
        (separator_rows_1, remaining_rows_1, child_map_1),
        (separator_rows_2, remaining_rows_2, child_map_2),
        (separator_rows_3, remaining_rows_3, child_map_3),
    )
    results = []
    for level_number in range(1, 4):
        sep_part, upd_part, child_maps = sections[level_number - 1]
        group_count = front_count * 2**level_number
        sep_count = SEP // group_count
        upd_count = UPD // group_count
        pair_bit = level_number - 1
        child_front = leaf_place >> pair_bit
        sibling_front = child_front ^ 1
        position = leaf_place % 2**level_number * front_count + front_place
        own_map = lax.dynamic_index_in_dim(child_maps, child_front, 0, keepdims=False)
        targets = owned_rows(position, group_count)
        sibling_map = lax.dynamic_index_in_dim(child_maps, sibling_front, 0, keepdims=False)
        sibling_full = from_partner(child_full, "leaf", pair_bit)
        sibling_block = select_rows(sibling_full, sibling_map, targets)
        own_term = expand_columns(select_rows(child_full, own_map, targets), own_map)
        sibling_term = expand_columns(sibling_block, sibling_map)
        is_odd = child_front & 1 == 1
        earlier_term = jnp.where(is_odd, sibling_term, own_term)
        later_term = jnp.where(is_odd, own_term, sibling_term)
        front_rows = jnp.concatenate([sep_part, upd_part], axis=0) + earlier_term + later_term
        panel_all = collect(front_rows[:, :SEP], level_number)
        blocks = panel_all.reshape(group_count, sep_count + upd_count, SEP)
        pivot_block = blocks[:, :sep_count].reshape(SEP, SEP)
        lower_block = blocks[:, sep_count:].reshape(UPD, SEP)
        diag_factor = jnp.linalg.cholesky(pivot_block)
        solved_all = lax.linalg.triangular_solve(
            diag_factor, lower_block, left_side=False, lower=True, transpose_a=True
        )
        solved_own = lax.dynamic_slice_in_dim(solved_all, position * upd_count, upd_count, 0)
        results.append(lax.dynamic_slice_in_dim(diag_factor, position * sep_count, sep_count, 0))
        results.append(solved_own)
        if level_number < 3:
            update_own = front_rows[sep_count:, SEP:] - jnp.dot(
                solved_own, solved_all.T, precision=lax.Precision.HIGHEST
            )
            child_full = collect(update_own, level_number)
    return (results[0], results[1], results[2], results[3], results[4], results[5])


def solution(mesh):
    in_specs = (
        P("leaf", None),
        P(("leaf", "front"), None),
        P(("leaf", "front"), None),
        P(("leaf", "front"), None),
        P(("leaf", "front"), None),
        P(("leaf", "front"), None),
        P(("leaf", "front"), None),
        P(),
        P(),
        P(),
    )
    out_specs = (
        P(("leaf", "front"), None),
        P(("leaf", "front"), None),
        P(("leaf", "front"), None),
        P(("leaf", "front"), None),
        P(("leaf", "front"), None),
        P(("leaf", "front"), None),
    )
    return jax.shard_map(body, mesh=mesh, in_specs=in_specs, out_specs=out_specs, check_vma=False)
```

profile of v0, /device:TPU:0, one launch (start us, length us, event | category | flops | bytes accessed | tf_op | source)
XLA Modules:
  0.0 1275.3 jit_solution(4523208993305382523)
XLA Ops:
  16.1 85.0 %collective-permute-done = f32[1024,1024]{1,0:T(8,128)} collective-permute-done((f32[1024,1024]{1,0:T(8,128)}, f32[1024,1024]{1,0:T(8,128)}, u32[]{:S(2)}, u32[]{:S(2)}) %collective-permute-start) | collective-permute-done | bytes 4194336 | tf_op jit(solution)/shard_map/ppermute | solution.py:21
  109.4 21.0 %all-gather.4.cloned.1.call-done = f32[768,512]{1,0:T(8,128)} async-done(((f32[192,512]{1,0:T(8,128)}), f32[768,512]{1,0:T(8,128)}) %all-gather.4.cloned.1.call-update) | async-done | bytes 1572880 | tf_op jit(solution)/shard_map/all_gather | solution.py:25
  131.9 35.3 %collective-permute-done.1 = f32[768,512]{1,0:T(8,128)S(1)} collective-permute-done((f32[768,512]{1,0:T(8,128)}, f32[768,512]{1,0:T(8,128)S(1)}, u32[]{:S(2)}, u32[]{:S(2)}) %collective-permute-start.1) | collective-permute-done | bytes 1572896 | tf_op jit(solution)/shard_map/ppermute | solution.py:21
  173.7 11.7 cholesky.374
  185.5 9.8 custom-call.31
  197.9 11.7 cholesky.393
  209.6 10.2 custom-call.32
  221.4 11.7 cholesky.414
  233.2 9.8 custom-call.33
  244.4 11.9 cholesky.431
  262.4 11.6 while.6
  274.0 39.3 %custom-call.34 = f32[4,128,128]{1,2,0:T(8,128)S(1)} custom-call(f32[4,128,128]{2,1,0:T(8,128)S(1)} %get-tuple-element.31), custom_call_target="InvertDiagBlocksLowerTriangular" | custom-call | tf_op jit(solution)/shard_map/triangular_solve/custom-call.3 | solution.py:115
  319.9 3.7 fusion
  328.9 22.3 %all-gather.6.cloned.1.call-done = f32[512,1024]{1,0:T(8,128)} async-done(((f32[128,1024]{1,0:T(8,128)}), f32[512,1024]{1,0:T(8,128)}) %all-gather.6.cloned.1.call-update) | async-done | bytes 2097168 | tf_op jit(solution)/shard_map/all_gather | solution.py:25
  352.7 46.5 %collective-permute-done.2 = f32[512,1024]{1,0:T(8,128)S(1)} collective-permute-done((f32[512,1024]{1,0:T(8,128)}, f32[512,1024]{1,0:T(8,128)S(1)}, u32[]{:S(2)}, u32[]{:S(2)}) %collective-permute-start.2) | collective-permute-done | bytes 2097184 | tf_op jit(solution)/shard_map/ppermute | solution.py:21
  399.2 5.1 maximum_select_fusion
  410.0 86.5 %collective-permute-done.3 = f32[1024,1024]{1,0:T(8,128)} collective-permute-done((f32[1024,1024]{1,0:T(8,128)}, f32[1024,1024]{1,0:T(8,128)}, u32[]{:S(2)}, u32[]{:S(2)}) %collective-permute-start.3) | collective-permute-done | bytes 4194336 | tf_op jit(solution)/shard_map/ppermute | solution.py:21
  501.2 7.4 all_gather.17
  510.3 18.1 %collective-permute-done.4 = f32[384,512]{1,0:T(8,128)S(1)} collective-permute-done((f32[384,512]{1,0:T(8,128)S(1)}, f32[384,512]{1,0:T(8,128)S(1)}, u32[]{:S(2)}, u32[]{:S(2)}) %collective-permute-start.4) | collective-permute-done | bytes 786464 | tf_op jit(solution)/shard_map/ppermute | solution.py:21
  530.4 34.1 %collective-permute-done.5 = f32[768,512]{1,0:T(8,128)S(1)} collective-permute-done((f32[768,512]{1,0:T(8,128)S(1)}, f32[768,512]{1,0:T(8,128)S(1)}, u32[]{:S(2)}, u32[]{:S(2)}) %collective-permute-start.5) | collective-permute-done | bytes 1572896 | tf_op jit(solution)/shard_map/ppermute | solution.py:21
  568.8 11.7 cholesky.446
  580.7 9.8 custom-call.35
  593.0 11.9 cholesky.465
  604.9 9.8 custom-call.36
  616.3 11.7 cholesky.486
  628.1 9.8 custom-call.37
  639.3 12.1 cholesky.503
  658.2 11.6 while.7
  669.8 39.3 %custom-call.38 = f32[4,128,128]{1,2,0:T(8,128)S(1)} custom-call(f32[4,128,128]{2,1,0:T(8,128)S(1)} %get-tuple-element.32), custom_call_target="InvertDiagBlocksLowerTriangular" | custom-call | tf_op jit(solution)/shard_map/triangular_solve/custom-call.3 | solution.py:115
  715.6 3.7 fusion.6
  723.5 18.0 %all-gather.8.cloned.1.call-done = f32[256,1024]{1,0:T(8,128)} async-done(((f32[64,1024]{1,0:T(8,128)}), f32[256,1024]{1,0:T(8,128)}) %all-gather.8.cloned.1.call-update) | async-done | bytes 1048592 | tf_op jit(solution)/shard_map/all_gather | solution.py:25
  743.0 24.0 %collective-permute-done.6 = f32[256,1024]{1,0:T(8,128)S(1)} collective-permute-done((f32[256,1024]{1,0:T(8,128)}, f32[256,1024]{1,0:T(8,128)S(1)}, u32[]{:S(2)}, u32[]{:S(2)}) %collective-permute-start.6) | collective-permute-done | bytes 1048608 | tf_op jit(solution)/shard_map/ppermute | solution.py:21
  770.4 45.5 %collective-permute-done.7 = f32[512,1024]{1,0:T(8,128)S(1)} collective-permute-done((f32[512,1024]{1,0:T(8,128)S(1)}, f32[512,1024]{1,0:T(8,128)S(1)}, u32[]{:S(2)}, u32[]{:S(2)}) %collective-permute-start.7) | collective-permute-done | bytes 2097184 | tf_op jit(solution)/shard_map/ppermute | solution.py:21
  824.5 175.8 %collective-permute-done.8 = f32[1024,1024]{1,0:T(8,128)} collective-permute-done((f32[1024,1024]{1,0:T(8,128)}, f32[1024,1024]{1,0:T(8,128)}, u32[]{:S(2)}, u32[]{:S(2)}) %collective-permute-start.8) | collective-permute-done | bytes 4194336 | tf_op jit(solution)/shard_map/ppermute | solution.py:21
  1004.3 6.3 all_gather.19
  1012.1 9.9 collective-permute-done.9
  1022.7 18.4 %collective-permute-done.10 = f32[384,512]{1,0:T(8,128)S(1)} collective-permute-done((f32[384,512]{1,0:T(8,128)S(1)}, f32[384,512]{1,0:T(8,128)S(1)}, u32[]{:S(2)}, u32[]{:S(2)}) %collective-permute-start.10) | collective-permute-done | bytes 786464 | tf_op jit(solution)/shard_map/ppermute | solution.py:21
  1049.1 61.7 %collective-permute-done.11 = f32[768,512]{1,0:T(8,128)S(1)} collective-permute-done((f32[768,512]{1,0:T(8,128)S(1)}, f32[768,512]{1,0:T(8,128)S(1)}, u32[]{:S(2)}, u32[]{:S(2)}) %collective-permute-start.11) | collective-permute-done | bytes 1572896 | tf_op jit(solution)/shard_map/ppermute | solution.py:21
  1115.2 11.7 cholesky.518
  1127.1 9.8 custom-call.39
  1139.4 11.9 cholesky.537
  1151.4 9.8 custom-call.40
  1162.7 11.7 cholesky.558
  1174.5 9.8 custom-call.41
  1185.7 11.9 cholesky.575
  1204.6 11.5 while.8
  1216.0 39.3 %custom-call.42 = f32[4,128,128]{1,2,0:T(8,128)S(1)} custom-call(f32[4,128,128]{2,1,0:T(8,128)S(1)} %get-tuple-element.33), custom_call_target="InvertDiagBlocksLowerTriangular" | custom-call | tf_op jit(solution)/shard_map/triangular_solve/custom-call.3 | solution.py:115
  1261.8 3.6 fusion.12
  (252 shorter events, 171.8 us)
Async XLA Ops:
  7.2 123.3 %all-gather.4.cloned.1.call-start = ((), (), s32[]{:S(2)}) async-start(), calls=%async_computation | async-start | bytes 1966080 | tf_op jit(solution)/shard_map/all_gather | solution.py:25
  7.2 93.9 %collective-permute-start = (f32[1024,1024]{1,0:T(8,128)}, f32[1024,1024]{1,0:T(8,128)}, u32[]{:S(2)}, u32[]{:S(2)}) collective-permute-start(f32[1024,1024]{1,0:T(8,128)} %param.19), channel_id=1, source_target_pairs={{0,4},{4,0},{8,12},{12,8},{16,20},{20,16},{24,28},{28,24},{1,5},{5... | collective-permute-start | bytes 12582920 | tf_op jit(solution)/shard_map/ppermute | solution.py:21
  104.9 1.1 copy-start.6
  104.9 1.2 copy-start.8
  107.3 1.0 copy-start.3
  109.1 242.1 %all-gather.6.cloned.1.call-start = ((), (), s32[]{:S(2)}) async-start(), calls=%async_computation.1 | async-start | bytes 2621440 | tf_op jit(solution)/shard_map/all_gather | solution.py:25
  130.5 36.7 %collective-permute-start.1 = (f32[768,512]{1,0:T(8,128)}, f32[768,512]{1,0:T(8,128)S(1)}, u32[]{:S(2)}, u32[]{:S(2)}) collective-permute-start(f32[768,512]{1,0:T(8,128)} %all-gather.4.cloned.1.call-done), channel_id=1, source_target_pairs={{0,4},{4,0},{8,12},{12,8},{16,20},{20,16},{24,28},{28,24},{1,5},{5... | collective-permute-start | bytes 4718600 | tf_op jit(solution)/shard_map/ppermute | solution.py:21
  172.7 1.0 copy-start
  324.5 0.7 copy-start.4
  328.4 77.4 %copy-start.13 = (s32[4,8]{1,0:T(4,128)S(1)}, s32[4,8]{1,0:T(4,128)}, u32[]{:S(2)}) copy-start(s32[4,8]{1,0:T(4,128)} %param.27) | copy-start | bytes 388
  328.5 413.0 %all-gather.8.cloned.1.call-start = ((), (), s32[]{:S(2)}) async-start(), calls=%async_computation.2 | async-start | bytes 1310720 | tf_op jit(solution)/shard_map/all_gather | solution.py:25
  351.2 48.0 %collective-permute-start.2 = (f32[512,1024]{1,0:T(8,128)}, f32[512,1024]{1,0:T(8,128)S(1)}, u32[]{:S(2)}, u32[]{:S(2)}) collective-permute-start(f32[512,1024]{1,0:T(8,128)} %all-gather.6.cloned.1.call-done), channel_id=1, source_target_pairs={{0,4},{4,0},{8,12},{12,8},{16,20},{20,16},{24,28},{28,24},{1,5},{5... | collective-permute-start | bytes 6291464 | tf_op jit(solution)/shard_map/ppermute | solution.py:21
  404.3 92.2 %collective-permute-start.3 = (f32[1024,1024]{1,0:T(8,128)}, f32[1024,1024]{1,0:T(8,128)}, u32[]{:S(2)}, u32[]{:S(2)}) collective-permute-start(f32[1024,1024]{1,0:T(8,128)} %maximum_select_fusion), channel_id=1, source_target_pairs={{0,8},{8,0},{4,12},{12,4},{16,24},{24,16},{20,28},{28,20},{1,9},{9... | collective-permute-start | bytes 12582920 | tf_op jit(solution)/shard_map/ppermute | solution.py:21
  499.6 1.0 copy-start.7
  499.6 1.0 copy-start.10
  501.2 9.2 copy-start.5
  508.6 19.8 %collective-permute-start.4 = (f32[384,512]{1,0:T(8,128)S(1)}, f32[384,512]{1,0:T(8,128)S(1)}, u32[]{:S(2)}, u32[]{:S(2)}) collective-permute-start(f32[384,512]{1,0:T(8,128)S(1)} %all_gather.17), channel_id=1, source_target_pairs={{0,4},{4,0},{8,12},{12,8},{16,20},{20,16},{24,28},{28,24},{1,5},{5... | collective-permute-start | bytes 2359304 | tf_op jit(solution)/shard_map/ppermute | solution.py:21
  528.6 35.9 %collective-permute-start.5 = (f32[768,512]{1,0:T(8,128)S(1)}, f32[768,512]{1,0:T(8,128)S(1)}, u32[]{:S(2)}, u32[]{:S(2)}) collective-permute-start(f32[768,512]{1,0:T(8,128)S(1)} %maximum_select_fusion.6), channel_id=1, source_target_pairs={{0,8},{8,0},{4,12},{12,4},{16,24},{24,16},{20,28},{28,20},{1,9},{9... | collective-permute-start | bytes 4718600 | tf_op jit(solution)/shard_map/ppermute | solution.py:21
  567.8 1.0 copy-start.1
  741.5 25.5 %collective-permute-start.6 = (f32[256,1024]{1,0:T(8,128)}, f32[256,1024]{1,0:T(8,128)S(1)}, u32[]{:S(2)}, u32[]{:S(2)}) collective-permute-start(f32[256,1024]{1,0:T(8,128)} %all-gather.8.cloned.1.call-done), channel_id=1, source_target_pairs={{0,4},{4,0},{8,12},{12,8},{16,20},{20,16},{24,28},{28,24},{1,5},{5... | collective-permute-start | bytes 3145736 | tf_op jit(solution)/shard_map/ppermute | solution.py:21
  768.8 51.9 %copy-start.12 = (s32[2,8]{1,0:T(2,128)S(1)}, s32[2,8]{1,0:T(2,128)}, u32[]{:S(2)}) copy-start(s32[2,8]{1,0:T(2,128)} %param.28) | copy-start | bytes 196
  768.9 47.0 %collective-permute-start.7 = (f32[512,1024]{1,0:T(8,128)S(1)}, f32[512,1024]{1,0:T(8,128)S(1)}, u32[]{:S(2)}, u32[]{:S(2)}) collective-permute-start(f32[512,1024]{1,0:T(8,128)S(1)} %maximum_select_fusion.5), channel_id=1, source_target_pairs={{0,8},{8,0},{4,12},{12,4},{16,24},{24,16},{20,28},{28,20},{1,9},{9... | collective-permute-start | bytes 6291464 | tf_op jit(solution)/shard_map/ppermute | solution.py:21
  818.2 182.1 %collective-permute-start.8 = (f32[1024,1024]{1,0:T(8,128)}, f32[1024,1024]{1,0:T(8,128)}, u32[]{:S(2)}, u32[]{:S(2)}) collective-permute-start(f32[1024,1024]{1,0:T(8,128)} %maximum_select_fusion.1), channel_id=1, source_target_pairs={{0,16},{16,0},{4,20},{20,4},{8,24},{24,8},{12,28},{28,12},{1,17},{... | collective-permute-start | bytes 12582920 | tf_op jit(solution)/shard_map/ppermute | solution.py:21
  1003.2 0.9 copy-start.9
  1003.2 1.0 copy-start.11
  1010.6 11.4 collective-permute-start.9
  1022.0 19.1 %collective-permute-start.10 = (f32[384,512]{1,0:T(8,128)S(1)}, f32[384,512]{1,0:T(8,128)S(1)}, u32[]{:S(2)}, u32[]{:S(2)}) collective-permute-start(f32[384,512]{1,0:T(8,128)S(1)} %maximum_select_fusion.8), channel_id=1, source_target_pairs={{0,8},{8,0},{4,12},{12,4},{16,24},{24,16},{20,28},{28,20},{1,9},{9... | collective-permute-start | bytes 2359304 | tf_op jit(solution)/shard_map/ppermute | solution.py:21
  1041.3 69.6 %collective-permute-start.11 = (f32[768,512]{1,0:T(8,128)S(1)}, f32[768,512]{1,0:T(8,128)S(1)}, u32[]{:S(2)}, u32[]{:S(2)}) collective-permute-start(f32[768,512]{1,0:T(8,128)S(1)} %maximum_select_fusion.7), channel_id=1, source_target_pairs={{0,16},{16,0},{4,20},{20,4},{8,24},{24,8},{12,28},{28,12},{1,17},{... | collective-permute-start | bytes 4718600 | tf_op jit(solution)/shard_map/ppermute | solution.py:21
  1114.2 1.0 copy-start.2
Sparse Core Ops, SparseCore 0:
  109.3 21.1 all-gather.3
  328.6 22.5 all-gather.5
  723.6 17.8 all-gather.7
where the time goes:
time: 1280 us
  waiting for transfers between devices  702 us (55%)
  other arithmetic  382 us (30%)
  local copies, waits for them, and re-layouts  74.1 us (6%)
  matrix products  59 us (5%)
  between operations  23 us (2%)
  starting transfers between devices  21.5 us (2%)
  blocking collectives  13.7 us (1%)
    ppermute x12, waiting for transfers between devices, from_partner(): return lax.ppermute(block, axis, route)  641 us
    another operation x44, other arithmetic, body(): diag_factor = jnp.linalg.cholesky(pivot_block)  238 us
    another operation x10, other arithmetic, body(): lax.linalg.triangular_solve(diag_factor, lower_block, left_side=False, lo...  123 us
    all_gather x3, waiting for transfers between devices, collect(): gathered = lax.all_gather(pieces, 'front', axis=0, tiled=True)  61.4 us
    another operation x40, local copies, waits for them, and re-layouts, body(): lax.linalg.triangular_solve(diag_factor, lower_block, left_side=False, lo...  34.4 us
    another operation x21, matrix products, body(): lax.linalg.triangular_solve(diag_factor, lower_block, left_side=False, lo...  32.4 us
  transfers between devices with their start and end apart: 15, of which 15 were waited for; matrix products, arithmetic and copies ran while one was open for 2% of the time, Pallas kernels for 0%

commit v1 on v0

--- a/solution.py
+++ b/solution.py
@@ -1,6 +1,10 @@
+import functools
+
 import jax
 import jax.numpy as jnp
 from jax import lax
+from jax.experimental import pallas as pl
+from jax.experimental.pallas import tpu as pltpu
 from jax.sharding import PartitionSpec as P
 
 TILE = 128
@@ -9,6 +13,119 @@
 NF = 1536
 NT = 12
 UT = 8
+STRIP = 8
+
+
+def split(value):
+    high = value.astype(jnp.bfloat16)
+    return high, (value - high.astype(jnp.float32)).astype(jnp.bfloat16)
+
+
+def dot3(left, right):
+    def one(a, b):
+        return lax.dot_general(a, b, (((1,), (1,)), ((), ())), preferred_element_type=jnp.float32)
+    return one(left[0], right[0]) + (one(left[0], right[1]) + one(left[1], right[0]))
+
+
+def invert_block(rows):
+    count = len(rows)
+    full = (STRIP, TILE)
+    lane = lax.broadcasted_iota(jnp.int32, full, 1)
+    sub = lax.broadcasted_iota(jnp.int32, full, 0)
+    out = []
+    for s in range(count):
+        base = s * STRIP
+        strip = rows[s]
+        cols = [jnp.broadcast_to(strip[:, base + j:base + j + 1], full) for j in range(STRIP)]
+        d = {(i, j): jnp.broadcast_to(cols[j][i:i + 1, :], full) for j in range(STRIP) for i in range(j, STRIP)}
+        in_strip = (lane >= base) & (lane < base + STRIP)
+        aug = jnp.where(in_strip, jnp.where(lane - base == sub, 1.0, 0.0), strip)
+        x = [jnp.broadcast_to(aug[i:i + 1, :], full) for i in range(STRIP)]
+        r = []
+        for k in range(STRIP):
+            r.append(lax.rsqrt(d[k, k]))
+            for i in range(k + 1, STRIP):
+                d[i, k] = d[i, k] * r[k]
+            for j in range(k + 1, STRIP):
+                for i in range(j, STRIP):
+                    d[i, j] = d[i, j] - d[i, k] * d[j, k]
+            x[k] = x[k] * r[k]
+            for i in range(k + 1, STRIP):
+                x[i] = x[i] - d[i, k] * x[k]
+        u = x[0]
+        for k in range(1, STRIP):
+            u = jnp.where(sub == k, x[k], u)
+        out.append(jnp.where(lane < base + STRIP, u, 0.0))
+        if s == count - 1:
+            break
+        v = list(x)
+        for k in range(STRIP - 1, -1, -1):
+            v[k] = v[k] * r[k]
+            for i in range(k):
+                v[i] = v[i] - d[k, i] * v[k]
+        for t in range(s + 1, count):
+            row = rows[t]
+            new = jnp.where(in_strip, 0.0, row)
+            for j in range(STRIP):
+                new = new - jnp.broadcast_to(row[:, base + j:base + j + 1], full) * v[j]
+            rows[t] = new
+    return out
+
+
+def factor_block(b, panel, work, inv, high, low):
+    total = panel.shape[0]
+    start = pl.multiple_of(b * TILE, TILE)
+    here = pl.ds(start, TILE)
+    done = dot3((high[...], low[...]), (high[here, :], low[here, :]))
+    work[...] = panel[:, here] - done
+    strips = [work[pl.ds(pl.multiple_of(start + STRIP * t, STRIP), STRIP), :] for t in range(TILE // STRIP)]
+    for t, strip in enumerate(invert_block(strips)):
+        inv[STRIP * t:STRIP * t + STRIP, :] = strip
+    column = dot3(split(work[...]), split(inv[...]))
+    row_ids = lax.broadcasted_iota(jnp.int32, (total, TILE), 0)
+    col_ids = lax.broadcasted_iota(jnp.int32, (total, TILE), 1) + start
+    column = jnp.where(row_ids >= col_ids, column, 0.0)
+    high_part, low_part = split(column)
+    high[:, here] = high_part
+    low[:, here] = low_part
+    return column
+
+
+def factor_kernel(pivot, below, diag, solved, panel, work, inv, high, low):
+    panel[:SEP, :] = pivot[...]
+    panel[SEP:, :] = below[...]
+    high[...] = jnp.zeros_like(high)
+    low[...] = jnp.zeros_like(low)
+
+    @pl.loop(0, SEP // TILE)
+    def _(b):
+        column = factor_block(b, panel, work, inv, high, low)
+        here = pl.ds(pl.multiple_of(b * TILE, TILE), TILE)
+        diag[:, here] = column[:SEP]
+        solved[:, here] = column[SEP:]
+
+
+def factor(pivot, below):
+    count = below.shape[0]
+    total = SEP + count
+    whole = pl.BlockSpec(memory_space=pltpu.VMEM)
+    return pl.pallas_call(
+        factor_kernel,
+        out_shape=(
+            jax.ShapeDtypeStruct((SEP, SEP), jnp.float32),
+            jax.ShapeDtypeStruct((count, SEP), jnp.float32),
+        ),
+        in_specs=[whole, whole],
+        out_specs=(whole, whole),
+        scratch_shapes=[
+            pltpu.VMEM((total, SEP), jnp.float32),
+            pltpu.VMEM((total, TILE), jnp.float32),
+            pltpu.VMEM((TILE, TILE), jnp.float32),
+            pltpu.VMEM((total, SEP), jnp.bfloat16),
+            pltpu.VMEM((total, SEP), jnp.bfloat16),
+        ],
+        compiler_params=pltpu.CompilerParams(vmem_limit_bytes=48 * 2**20),
+    )(pivot, below)
 
 
 def from_partner(block, axis, stride):
@@ -59,10 +176,14 @@
 
 
 def expand_columns(row_block, tile_map):
-    placing = (tile_map[:, None] == jnp.arange(NT, dtype=jnp.int32)[None, :]).astype(jnp.float32)
-    tiled = row_block.reshape(row_block.shape[0], UT, TILE)
-    placed = jnp.einsum("rut,un->rnt", tiled, placing, precision=lax.Precision.HIGHEST)
-    return placed.reshape(row_block.shape[0], NF)
+    placing = tile_map[:, None] == jnp.arange(NT, dtype=jnp.int32)[None, :]
+    placed = []
+    for n in range(NT):
+        total = jnp.zeros((row_block.shape[0], TILE), jnp.float32)
+        for u in range(UT):
+            total = jnp.where(placing[u, n], row_block[:, u * TILE:(u + 1) * TILE], total)
+        placed.append(total)
+    return jnp.concatenate(placed, axis=1)
 
 
 def body(
@@ -96,55 +217,38 @@
         child_front = leaf_place >> pair_bit
         sibling_front = child_front ^ 1
         position = leaf_place % 2**level_number * front_count + front_place
+        partner = (leaf_place ^ 1 << pair_bit) % 2**level_number * front_count + front_place
         own_map = lax.dynamic_index_in_dim(child_maps, child_front, 0, keepdims=False)
+        sibling_map = lax.dynamic_index_in_dim(child_maps, sibling_front, 0, keepdims=False)
         targets = owned_rows(position, group_count)
-        sibling_map = lax.dynamic_index_in_dim(child_maps, sibling_front, 0, keepdims=False)
-        sibling_full = from_partner(child_full, "leaf", pair_bit)
-        sibling_block = select_rows(sibling_full, sibling_map, targets)
+        for_partner = select_rows(child_full, own_map, owned_rows(partner, group_count))
+        sibling_block = from_partner(for_partner, "leaf", pair_bit)
         own_term = expand_columns(select_rows(child_full, own_map, targets), own_map)
         sibling_term = expand_columns(sibling_block, sibling_map)
-        is_odd = child_front & 1 == 1
-        earlier_term = jnp.where(is_odd, sibling_term, own_term)
-        later_term = jnp.where(is_odd, own_term, sibling_term)
-        front_rows = jnp.concatenate([sep_part, upd_part], axis=0) + earlier_term + later_term
-        panel_all = collect(front_rows[:, :SEP], level_number)
-        blocks = panel_all.reshape(group_count, sep_count + upd_count, SEP)
-        pivot_block = blocks[:, :sep_count].reshape(SEP, SEP)
-        lower_block = blocks[:, sep_count:].reshape(UPD, SEP)
-        diag_factor = jnp.linalg.cholesky(pivot_block)
-        solved_all = lax.linalg.triangular_solve(
-            diag_factor, lower_block, left_side=False, lower=True, transpose_a=True
-        )
-        solved_own = lax.dynamic_slice_in_dim(solved_all, position * upd_count, upd_count, 0)
+        front_rows = jnp.concatenate([sep_part, upd_part], axis=0) + own_term + sibling_term
+        if level_number < 3:
+            panel_all = collect(front_rows[:, :SEP], level_number)
+            blocks = panel_all.reshape(group_count, sep_count + upd_count, SEP)
+            pivot_block = blocks[:, :sep_count].reshape(SEP, SEP)
+            lower_block = blocks[:, sep_count:].reshape(UPD, SEP)
+        else:
+            pivot_block = collect(front_rows[:sep_count, :SEP], level_number)
+            lower_block = front_rows[sep_count:, :SEP]
+        diag_factor, solved_all = factor(pivot_block, lower_block)
         results.append(lax.dynamic_slice_in_dim(diag_factor, position * sep_count, sep_count, 0))
-        results.append(solved_own)
         if level_number < 3:
+            solved_own = lax.dynamic_slice_in_dim(solved_all, position * upd_count, upd_count, 0)
+            results.append(solved_own)
             update_own = front_rows[sep_count:, SEP:] - jnp.dot(
                 solved_own, solved_all.T, precision=lax.Precision.HIGHEST
             )
             child_full = collect(update_own, level_number)
-    return (results[0], results[1], results[2], results[3], results[4], results[5])
+        else:
+            results.append(solved_all)
+    return tuple(results)
 
 
 def solution(mesh):
-    in_specs = (
-        P("leaf", None),
-        P(("leaf", "front"), None),
-        P(("leaf", "front"), None),
-        P(("leaf", "front"), None),
-        P(("leaf", "front"), None),
-        P(("leaf", "front"), None),
-        P(("leaf", "front"), None),
-        P(),
-        P(),
-        P(),
-    )
-    out_specs = (
-        P(("leaf", "front"), None),
-        P(("leaf", "front"), None),
-        P(("leaf", "front"), None),
-        P(("leaf", "front"), None),
-        P(("leaf", "front"), None),
-        P(("leaf", "front"), None),
-    )
-    return jax.shard_map(body, mesh=mesh, in_specs=in_specs, out_specs=out_specs, check_vma=False)
+    rows = P(("leaf", "front"), None)
+    in_specs = (P("leaf", None),) + (rows,) * 6 + (P(),) * 3
+    return jax.shard_map(body, mesh=mesh, in_specs=in_specs, out_specs=(rows,) * 6, check_vma=False)

time: 1280 us -> 858 us (0.67)
  waiting for transfers between devices: 702 us -> 280 us
  Pallas kernels: 0 us -> 88.3 us
  matrix products: 59 us -> 5.93 us
  local copies, waits for them, and re-layouts: 74.1 us -> 51 us
    ppermute x12, waiting for transfers between devices: 641 us -> 221 us  [from_partner(): return lax.ppermute(block, axis, route)]
    another operation x54 -> x0, other arithmetic: 361 us -> none  [the longest x44 238 us: body(): diag_factor = jnp.linalg.cholesky(pivot_block)]
    unnamed x6 -> x66, other arithmetic: 0.72 us -> 331 us
    pallas_call x0 -> x3, Pallas kernels: none -> 88.3 us  [factor(): pl.pallas_call(factor_kernel, out_shape=(jax.ShapeDtypeStruct((SEP, SEP),...]
    another operation x39 -> x0, matrix products: 48.8 us -> none  [the longest x21 32.4 us: body(): lax.linalg.triangular_solve(diag_factor, lower_block, left_side=False, lo...]
    another operation x52 -> x0, local copies, waits for them, and re-layouts: 34.8 us -> none  [the longest x40 34.4 us: body(): lax.linalg.triangular_solve(diag_factor, lower_block, left_side=False, lo...]
    concatenate x0 -> x6, other arithmetic: none -> 30 us  [expand_columns(): return jnp.concatenate(placed, axis=1)]
    slice x0 -> x38, local copies, waits for them, and re-layouts: none -> 25.1 us  [the longest x36 25.1 us: expand_columns(): placing[u, n]]
  transfers between devices with their start and end apart: 15 -> 15, of which waited for: 15 -> 12; matrix products, arithmetic and copies ran while one was open for 2% -> 25% of each run, Pallas kernels for 0% -> 0%
where the time goes in v1:
time: 858 us; the launch traced here: 852 us
  other arithmetic  380 us (44%)
  waiting for transfers between devices  280 us (33%)
  Pallas kernels  88.3 us (10%)
  local copies, waits for them, and re-layouts  51 us (6%)
  starting transfers between devices  19 us (2%)
  between operations  15 us (2%)
  blocking collectives  13.1 us (2%)
    unnamed x66, other arithmetic  331 us
    ppermute x12, waiting for transfers between devices, from_partner(): return lax.ppermute(block, axis, route)  221 us
    pallas_call x3, Pallas kernels, factor(): pl.pallas_call(factor_kernel, out_shape=(jax.ShapeDtypeStruct((SEP, SEP),...  88.3 us
    all_gather x3, waiting for transfers between devices, collect(): gathered = lax.all_gather(pieces, 'front', axis=0, tiled=True)  59.1 us
    concatenate x6, other arithmetic, expand_columns(): return jnp.concatenate(placed, axis=1)  30 us
    slice x36, local copies, waits for them, and re-layouts, expand_columns(): placing[u, n]  25.1 us
    gather x6, local copies, waits for them, and re-layouts, select_rows(): jnp.take(full_update, source, axis=0)  19 us
    ppermute x12, starting transfers between devices, from_partner(): return lax.ppermute(block, axis, route)  18.5 us
  transfers between devices with their start and end apart: 15, of which 12 were waited for; matrix products, arithmetic and copies ran while one was open for 25% of the time, Pallas kernels for 0%

profile of v1, /device:TPU:0, one launch (start us, length us, event | category | flops | bytes accessed | tf_op | source)
XLA Modules:
  0.0 852.0 jit_solution(10731724138771959128)
XLA Ops:
  26.7 5.0 constant_dynamic-update-slice_fusion.11
  46.5 5.2 constant_dynamic-update-slice_fusion.7
  51.7 5.0 constant_dynamic-update-slice_fusion.6
  56.8 5.1 constant_dynamic-update-slice_fusion.5
  72.6 5.1 constant_dynamic-update-slice_fusion.2
  77.7 5.0 constant_dynamic-update-slice_fusion.1
  87.7 5.1 constant_dynamic-update-slice_fusion.23
  97.8 5.1 constant_dynamic-update-slice_fusion.21
  117.9 5.0 constant_dynamic-update-slice_fusion.17
  122.9 5.1 constant_dynamic-update-slice_fusion.16
  128.0 5.1 constant_dynamic-update-slice_fusion.15
  133.1 5.2 constant_dynamic-update-slice_fusion.14
  149.5 19.9 %all-gather.4.cloned.1.call-done = f32[768,512]{1,0:T(8,128)} async-done(((f32[192,512]{1,0:T(8,128)}), f32[768,512]{1,0:T(8,128)}) %all-gather.4.cloned.1.call-update) | async-done | bytes 1572880 | tf_op jit(solution)/shard_map/all_gather | solution.py:142
  170.9 35.4 %collective-permute-done.1 = f32[768,512]{1,0:T(8,128)} collective-permute-done((f32[768,512]{1,0:T(8,128)}, f32[768,512]{1,0:T(8,128)}, u32[]{:S(2)}, u32[]{:S(2)}) %collective-permute-start.1) | collective-permute-done | bytes 1572896 | tf_op jit(solution)/shard_map/ppermute | solution.py:138
  211.5 31.6 %shard_map.145 = (f32[512,512]{1,0:T(8,128)S(1)}, f32[1024,512]{1,0:T(8,128)S(1)}) custom-call(f32[512,512]{1,0:T(8,128)S(1)} %bitcast.598, f32[1024,512]{1,0:T(8,128)} %bitcast.604), custom_call_target="tpu_custom_call" | custom-call | tf_op jit(solution)/shard_map/pallas_call | solution.py:112
  246.7 22.3 %all-gather.6.cloned.1.call-done = f32[512,1024]{1,0:T(8,128)} async-done(((f32[128,1024]{1,0:T(8,128)}), f32[512,1024]{1,0:T(8,128)}) %all-gather.6.cloned.1.call-update) | async-done | bytes 2097168 | tf_op jit(solution)/shard_map/all_gather | solution.py:142
  279.2 37.7 %collective-permute-done.2 = f32[512,1024]{1,0:T(8,128)S(1)} collective-permute-done((f32[512,1024]{1,0:T(8,128)}, f32[512,1024]{1,0:T(8,128)S(1)}, u32[]{:S(2)}, u32[]{:S(2)}) %collective-permute-start.2) | collective-permute-done | bytes 2097184 | tf_op jit(solution)/shard_map/ppermute | solution.py:138
  317.0 5.1 maximum_select_fusion
  360.0 5.1 constant_dynamic-update-slice_fusion.29
  384.4 5.1 constant_dynamic-update-slice_fusion.24
  389.5 5.2 constant_dynamic-update-slice_fusion.47
  394.8 5.1 constant_dynamic-update-slice_fusion.46
  399.9 5.2 constant_dynamic-update-slice_fusion.45
  405.1 5.0 constant_dynamic-update-slice_fusion.44
  415.0 5.2 constant_dynamic-update-slice_fusion.42
  425.1 5.2 constant_dynamic-update-slice_fusion.40
  435.3 5.1 constant_dynamic-update-slice_fusion.38
  445.3 5.2 constant_dynamic-update-slice_fusion.36
  450.6 7.7 all_gather.17
  459.8 18.3 %collective-permute-done.4 = f32[384,512]{1,0:T(8,128)S(1)} collective-permute-done((f32[384,512]{1,0:T(8,128)S(1)}, f32[384,512]{1,0:T(8,128)S(1)}, u32[]{:S(2)}, u32[]{:S(2)}) %collective-permute-start.4) | collective-permute-done | bytes 786464 | tf_op jit(solution)/shard_map/ppermute | solution.py:138
  478.7 35.6 %collective-permute-done.5 = f32[768,512]{1,0:T(8,128)} collective-permute-done((f32[768,512]{1,0:T(8,128)S(1)}, f32[768,512]{1,0:T(8,128)}, u32[]{:S(2)}, u32[]{:S(2)}) %collective-permute-start.5) | collective-permute-done | bytes 1572896 | tf_op jit(solution)/shard_map/ppermute | solution.py:138
  518.5 31.8 %shard_map.146 = (f32[512,512]{1,0:T(8,128)S(1)}, f32[1024,512]{1,0:T(8,128)S(1)}) custom-call(f32[512,512]{1,0:T(8,128)S(1)} %bitcast.599, f32[1024,512]{1,0:T(8,128)} %bitcast.605), custom_call_target="tpu_custom_call" | custom-call | tf_op jit(solution)/shard_map/pallas_call | solution.py:112
  553.2 16.9 %all-gather.8.cloned.1.call-done = f32[256,1024]{1,0:T(8,128)} async-done(((f32[64,1024]{1,0:T(8,128)}), f32[256,1024]{1,0:T(8,128)}) %all-gather.8.cloned.1.call-update) | async-done | bytes 1048592 | tf_op jit(solution)/shard_map/all_gather | solution.py:142
  571.7 23.9 %collective-permute-done.6 = f32[256,1024]{1,0:T(8,128)S(1)} collective-permute-done((f32[256,1024]{1,0:T(8,128)}, f32[256,1024]{1,0:T(8,128)S(1)}, u32[]{:S(2)}, u32[]{:S(2)}) %collective-permute-start.6) | collective-permute-done | bytes 1048608 | tf_op jit(solution)/shard_map/ppermute | solution.py:138
  607.7 36.7 %collective-permute-done.7 = f32[512,1024]{1,0:T(8,128)S(1)} collective-permute-done((f32[512,1024]{1,0:T(8,128)S(1)}, f32[512,1024]{1,0:T(8,128)S(1)}, u32[]{:S(2)}, u32[]{:S(2)}) %collective-permute-start.7) | collective-permute-done | bytes 2097184 | tf_op jit(solution)/shard_map/ppermute | solution.py:138
  655.4 5.1 constant_dynamic-update-slice_fusion.59
  665.5 5.2 constant_dynamic-update-slice_fusion.57
  675.7 5.2 constant_dynamic-update-slice_fusion.55
  680.9 5.0 constant_dynamic-update-slice_fusion.54
  720.8 5.1 constant_dynamic-update-slice_fusion.70
  725.8 5.1 constant_dynamic-update-slice_fusion.69
  735.9 5.0 constant_dynamic-update-slice_fusion.67
  751.0 5.1 constant_dynamic-update-slice_fusion.64
  766.1 5.1 constant_dynamic-update-slice_fusion.61
  776.1 5.4 all_gather.19
  788.8 6.3 collective-permute-done.10
  797.1 22.8 %collective-permute-done.11 = f32[256,512]{1,0:T(8,128)S(1)} collective-permute-done((f32[256,512]{1,0:T(8,128)S(1)}, f32[256,512]{1,0:T(8,128)S(1)}, u32[]{:S(2)}, u32[]{:S(2)}) %collective-permute-start.11) | collective-permute-done | bytes 524320 | tf_op jit(solution)/shard_map/ppermute | solution.py:138
  819.9 25.0 %shard_map.147 = (f32[512,512]{1,0:T(8,128)S(1)}, f32[32,512]{1,0:T(8,128)}) custom-call(f32[512,512]{1,0:T(8,128)S(1)} %maximum_select_fusion.6.pivot, f32[32,512]{1,0:T(8,128)S(1)} %slice.3133.below), custom_call_target="tpu_custom_call" | custom-call | tf_op jit(solution)/shard_map/pallas_call | solution.py:112
  (196 shorter events, 296.5 us)
Async XLA Ops:
  7.2 162.2 %all-gather.4.cloned.1.call-start = ((), (), s32[]{:S(2)}) async-start(), calls=%async_computation | async-start | bytes 1966080 | tf_op jit(solution)/shard_map/all_gather | solution.py:142
  12.2 75.5 %collective-permute-start = (f32[192,1024]{1,0:T(8,128)S(1)}, f32[192,1024]{1,0:T(8,128)S(1)}, u32[]{:S(2)}, u32[]{:S(2)}) collective-permute-start(f32[192,1024]{1,0:T(8,128)S(1)} %select_select_fusion), channel_id=1, source_target_pairs={{0,4},{4,0},{8,12},{12,8},{16,20},{20,16},{24,28},{28,24},{1,5},{5... | collective-permute-start | bytes 2359304 | tf_op jit(solution)/shard_map/ppermute | solution.py:138
  133.1 15.1 %copy-start.1 = (f32[128,1536]{1,0:T(8,128)S(1)}, f32[128,1536]{1,0:T(8,128)}, u32[]{:S(2)}) copy-start(f32[128,1536]{1,0:T(8,128)} %param.18) | copy-start | bytes 2359300
  133.1 15.1 %copy-start.3 = (f32[64,1536]{1,0:T(8,128)S(1)}, f32[64,1536]{1,0:T(8,128)}, u32[]{:S(2)}) copy-start(f32[64,1536]{1,0:T(8,128)} %param.17) | copy-start | bytes 1179652
  149.3 119.7 %all-gather.6.cloned.1.call-start = ((), (), s32[]{:S(2)}) async-start(), calls=%async_computation.1 | async-start | bytes 2621440 | tf_op jit(solution)/shard_map/all_gather | solution.py:142
  169.4 36.9 %collective-permute-start.1 = (f32[768,512]{1,0:T(8,128)}, f32[768,512]{1,0:T(8,128)}, u32[]{:S(2)}, u32[]{:S(2)}) collective-permute-start(f32[768,512]{1,0:T(8,128)} %all-gather.4.cloned.1.call-done), channel_id=1, source_target_pairs={{0,4},{4,0},{8,12},{12,8},{16,20},{20,16},{24,28},{28,24},{1,5},{5... | collective-permute-start | bytes 4718600 | tf_op jit(solution)/shard_map/ppermute | solution.py:138
  243.1 3.1 copy-start
  243.1 3.5 copy-start.9
  246.2 323.9 %all-gather.8.cloned.1.call-start = ((), (), s32[]{:S(2)}) async-start(), calls=%async_computation.2 | async-start | bytes 1310720 | tf_op jit(solution)/shard_map/all_gather | solution.py:142
  269.0 48.0 %collective-permute-start.2 = (f32[512,1024]{1,0:T(8,128)}, f32[512,1024]{1,0:T(8,128)S(1)}, u32[]{:S(2)}, u32[]{:S(2)}) collective-permute-start(f32[512,1024]{1,0:T(8,128)} %all-gather.6.cloned.1.call-done), channel_id=1, source_target_pairs={{0,4},{4,0},{8,12},{12,8},{16,20},{20,16},{24,28},{28,24},{1,5},{5... | collective-permute-start | bytes 6291464 | tf_op jit(solution)/shard_map/ppermute | solution.py:138
  325.3 64.2 %collective-permute-start.3 = (f32[96,1024]{1,0:T(8,128)S(1)}, f32[96,1024]{1,0:T(8,128)S(1)}, u32[]{:S(2)}, u32[]{:S(2)}) collective-permute-start(f32[96,1024]{1,0:T(8,128)S(1)} %select_select_fusion.2), channel_id=1, source_target_pairs={{0,8},{8,0},{4,12},{12,4},{16,24},{24,16},{20,28},{28,20},{1,9},{9... | collective-permute-start | bytes 1179656 | tf_op jit(solution)/shard_map/ppermute | solution.py:138
  415.0 35.5 %copy-start.4 = (f32[64,1536]{1,0:T(8,128)S(1)}, f32[64,1536]{1,0:T(8,128)}, u32[]{:S(2)}) copy-start(f32[64,1536]{1,0:T(8,128)} %param.20) | copy-start | bytes 1179652
  415.0 35.5 %copy-start.5 = (f32[32,1536]{1,0:T(8,128)S(1)}, f32[32,1536]{1,0:T(8,128)}, u32[]{:S(2)}) copy-start(f32[32,1536]{1,0:T(8,128)} %param.19) | copy-start | bytes 589828
  458.3 19.8 %collective-permute-start.4 = (f32[384,512]{1,0:T(8,128)S(1)}, f32[384,512]{1,0:T(8,128)S(1)}, u32[]{:S(2)}, u32[]{:S(2)}) collective-permute-start(f32[384,512]{1,0:T(8,128)S(1)} %all_gather.17), channel_id=1, source_target_pairs={{0,4},{4,0},{8,12},{12,8},{16,20},{20,16},{24,28},{28,24},{1,5},{5... | collective-permute-start | bytes 2359304 | tf_op jit(solution)/shard_map/ppermute | solution.py:138
  478.3 36.0 %collective-permute-start.5 = (f32[768,512]{1,0:T(8,128)S(1)}, f32[768,512]{1,0:T(8,128)}, u32[]{:S(2)}, u32[]{:S(2)}) collective-permute-start(f32[768,512]{1,0:T(8,128)S(1)} %maximum_select_fusion.5), channel_id=1, source_target_pairs={{0,8},{8,0},{4,12},{12,4},{16,24},{24,16},{20,28},{28,20},{1,9},{9... | collective-permute-start | bytes 4718600 | tf_op jit(solution)/shard_map/ppermute | solution.py:138
  550.3 2.9 copy-start.2
  550.4 21.2 %copy-start.8 = (s32[2,8]{1,0:T(2,128)S(1)}, s32[2,8]{1,0:T(2,128)}, u32[]{:S(2)}) copy-start(s32[2,8]{1,0:T(2,128)} %param.25) | copy-start | bytes 196
  570.1 25.5 %collective-permute-start.6 = (f32[256,1024]{1,0:T(8,128)}, f32[256,1024]{1,0:T(8,128)S(1)}, u32[]{:S(2)}, u32[]{:S(2)}) collective-permute-start(f32[256,1024]{1,0:T(8,128)} %all-gather.8.cloned.1.call-done), channel_id=1, source_target_pairs={{0,4},{4,0},{8,12},{12,8},{16,20},{20,16},{24,28},{28,24},{1,5},{5... | collective-permute-start | bytes 3145736 | tf_op jit(solution)/shard_map/ppermute | solution.py:138
  597.5 47.0 %collective-permute-start.7 = (f32[512,1024]{1,0:T(8,128)S(1)}, f32[512,1024]{1,0:T(8,128)S(1)}, u32[]{:S(2)}, u32[]{:S(2)}) collective-permute-start(f32[512,1024]{1,0:T(8,128)S(1)} %maximum_select_fusion.4), channel_id=1, source_target_pairs={{0,8},{8,0},{4,12},{12,4},{16,24},{24,16},{20,28},{28,20},{1,9},{9... | collective-permute-start | bytes 6291464 | tf_op jit(solution)/shard_map/ppermute | solution.py:138
  649.9 65.9 %collective-permute-start.8 = (f32[48,1024]{1,0:T(8,128)S(1)}, f32[48,1024]{1,0:T(8,128)S(1)}, u32[]{:S(2)}, u32[]{:S(2)}) collective-permute-start(f32[48,1024]{1,0:T(8,128)S(1)} %select_select_fusion.4), channel_id=1, source_target_pairs={{0,16},{16,0},{4,20},{20,4},{8,24},{24,8},{12,28},{28,12},{1,17},{... | collective-permute-start | bytes 589832 | tf_op jit(solution)/shard_map/ppermute | solution.py:138
  715.8 60.3 %copy-start.6 = (f32[32,1536]{1,0:T(8,128)S(1)}, f32[32,1536]{1,0:T(8,128)}, u32[]{:S(2)}) copy-start(f32[32,1536]{1,0:T(8,128)} %param.22) | copy-start | bytes 589828
  715.8 60.3 %copy-start.7 = (f32[16,1536]{1,0:T(8,128)S(1)}, f32[16,1536]{1,0:T(8,128)}, u32[]{:S(2)}) copy-start(f32[16,1536]{1,0:T(8,128)} %param.21) | copy-start | bytes 294916
  781.5 5.7 collective-permute-start.9
  787.3 7.8 collective-permute-start.10
  795.2 24.7 %collective-permute-start.11 = (f32[256,512]{1,0:T(8,128)S(1)}, f32[256,512]{1,0:T(8,128)S(1)}, u32[]{:S(2)}, u32[]{:S(2)}) collective-permute-start(f32[256,512]{1,0:T(8,128)S(1)} %maximum_select_fusion.7), channel_id=1, source_target_pairs={{0,16},{16,0},{4,20},{20,4},{8,24},{24,8},{12,28},{28,12},{1,17},{... | collective-permute-start | bytes 1572872 | tf_op jit(solution)/shard_map/ppermute | solution.py:138
Sparse Core Ops, SparseCore 0:
  149.4 19.9 all-gather.3
  246.4 22.5 all-gather.5
  553.4 16.6 all-gather.7

commit v2 on v1

v2 whole, which is shorter than its diff:
```python
import functools

import jax
import jax.numpy as jnp
from jax import lax
from jax.experimental import pallas as pl
from jax.experimental.pallas import tpu as pltpu
from jax.sharding import PartitionSpec as P

TILE = 128
SEP = 512
UPD = 1024
NF = 1536
NT = 12
UT = 8
STRIP = 8
MESH = pl.DeviceIdType.MESH
WHOLE = pl.BlockSpec(memory_space=pltpu.VMEM)
SCALARS = pl.BlockSpec(memory_space=pltpu.SMEM)


def split(value):
    high = value.astype(jnp.bfloat16)
    return high, (value - high.astype(jnp.float32)).astype(jnp.bfloat16)


def dot3(left, right):
    def one(a, b):
        return lax.dot_general(a, b, (((1,), (1,)), ((), ())), preferred_element_type=jnp.float32)
    return one(left[0], right[0]) + (one(left[0], right[1]) + one(left[1], right[0]))


def invert_block(rows):
    count = len(rows)
    full = (STRIP, TILE)
    lane = lax.broadcasted_iota(jnp.int32, full, 1)
    sub = lax.broadcasted_iota(jnp.int32, full, 0)
    out = []
    for s in range(count):
        base = s * STRIP
        strip = rows[s]
        cols = [jnp.broadcast_to(strip[:, base + j:base + j + 1], full) for j in range(STRIP)]
        d = {(i, j): jnp.broadcast_to(cols[j][i:i + 1, :], full) for j in range(STRIP) for i in range(j, STRIP)}
        in_strip = (lane >= base) & (lane < base + STRIP)
        aug = jnp.where(in_strip, jnp.where(lane - base == sub, 1.0, 0.0), strip)
        x = [jnp.broadcast_to(aug[i:i + 1, :], full) for i in range(STRIP)]
        r = []
        for k in range(STRIP):
            r.append(lax.rsqrt(d[k, k]))
            for i in range(k + 1, STRIP):
                d[i, k] = d[i, k] * r[k]
            for j in range(k + 1, STRIP):
                for i in range(j, STRIP):
                    d[i, j] = d[i, j] - d[i, k] * d[j, k]
            x[k] = x[k] * r[k]
            for i in range(k + 1, STRIP):
                x[i] = x[i] - d[i, k] * x[k]
        u = x[0]
        for k in range(1, STRIP):
            u = jnp.where(sub == k, x[k], u)
        out.append(jnp.where(lane < base + STRIP, u, 0.0))
        if s == count - 1:
            break
        v = list(x)
        for k in range(STRIP - 1, -1, -1):
            v[k] = v[k] * r[k]
            for i in range(k):
                v[i] = v[i] - d[k, i] * v[k]
        for t in range(s + 1, count):
            row = rows[t]
            new = jnp.where(in_strip, 0.0, row)
            for j in range(STRIP):
                new = new - jnp.broadcast_to(row[:, base + j:base + j + 1], full) * v[j]
            rows[t] = new
    return out


def factor_block(b, pivot, below, work, inv, high, low):
    total = work.shape[0]
    start = pl.multiple_of(b * TILE, TILE)
    here = pl.ds(start, TILE)
    done = dot3((high[...], low[...]), (high[here, :], low[here, :]))
    work[:SEP, :] = pivot[:, here] - done[:SEP]
    work[SEP:, :] = below[:, here] - done[SEP:]
    strips = [work[pl.ds(pl.multiple_of(start + STRIP * t, STRIP), STRIP), :] for t in range(TILE // STRIP)]
    for t, strip in enumerate(invert_block(strips)):
        inv[STRIP * t:STRIP * t + STRIP, :] = strip
    column = dot3(split(work[...]), split(inv[...]))
    row_ids = lax.broadcasted_iota(jnp.int32, (total, TILE), 0)
    col_ids = lax.broadcasted_iota(jnp.int32, (total, TILE), 1) + start
    column = jnp.where(row_ids >= col_ids, column, 0.0)
    high_part, low_part = split(column)
    high[:, here] = high_part
    low[:, here] = low_part
    return column


def child_piece(table, row, count):
    tile = lax.div(row, jnp.int32(TILE))
    here = pl.multiple_of(table[tile] * TILE + lax.rem(row, jnp.int32(TILE)), 8)
    return here, table[NT + tile].astype(jnp.float32)


def spread(table, rows, here, count, present, n):
    there = pl.ds(pl.multiple_of(table[n] * TILE, TILE), TILE)
    return rows[pl.ds(here, count), there] * (present * table[NT + n].astype(jnp.float32))


def assemble(table, own, other, child_rows, sep, upd, own_sep, own_upd, out_sep, out_upd):
    for out, size, offset, place, entries in (
        (out_sep, sep.shape[0], 0, other, None),
        (own_sep, sep.shape[0], 0, own, sep),
        (out_upd, upd.shape[0], SEP, other, None),
        (own_upd, upd.shape[0], SEP, own, upd),
    ):
        here, present = child_piece(table, offset + place * size, size)
        rows, here = child_rows(here, size)
        for n in range(out.shape[1] // TILE):
            cols = slice(n * TILE, (n + 1) * TILE)
            value = spread(table, rows, here, size, present, n)
            out[:, cols] = value if entries is None else value + entries[:, cols]


def assemble_kernel(place, table, leaf, sep, upd, *outs):
    assemble(table, place[0], place[1], lambda here, size: (leaf, here), sep, upd, *outs)


def assembled_shapes(sep, upd, level):
    width = SEP if level == 3 else NF
    sep_shape = jax.ShapeDtypeStruct((sep.shape[0], SEP), jnp.float32)
    upd_shape = jax.ShapeDtypeStruct((upd.shape[0], width), jnp.float32)
    return [sep_shape, upd_shape, sep_shape, upd_shape]


def assemble_leaf(place, table, leaf, sep, upd):
    shapes = assembled_shapes(sep, upd, 1)
    return pl.pallas_call(
        assemble_kernel,
        out_shape=tuple(shapes),
        in_specs=[SCALARS] * 2 + [WHOLE] * 3,
        out_specs=(WHOLE,) * 4,
        compiler_params=pltpu.CompilerParams(vmem_limit_bytes=32 * 2**20),
    )(place, table, leaf, sep, upd)


def factor_kernel(with_update, place, pivot, below, *refs):
    if with_update:
        rest, table, sep, upd, diag, solved, *outs = refs
        outs, refs = outs[:4], outs[4:]
        full_diag, full_solved, work, inv, high, low, child = refs
    else:
        diag, solved, full_diag, full_solved, work, inv, high, low = refs
    high[...] = jnp.zeros_like(high)
    low[...] = jnp.zeros_like(low)

    @pl.loop(0, SEP // TILE)
    def _(b):
        column = factor_block(b, pivot, below, work, inv, high, low)
        here = pl.ds(pl.multiple_of(b * TILE, TILE), TILE)
        full_diag[:, here] = column[:SEP]
        full_solved[:, here] = column[SEP:]

    sep_count = diag.shape[0]
    diag[...] = full_diag[pl.ds(pl.multiple_of(place[0] * sep_count, 8), sep_count), :]
    if not with_update:
        solved[...] = full_solved[...]
        return
    upd_count = solved.shape[0]
    solved[...] = full_solved[pl.ds(pl.multiple_of(place[0] * upd_count, 8), upd_count), :]

    def update_rows(here, size):
        left = split(full_solved[pl.ds(here, size), :])
        child[:size, :] = rest[pl.ds(here, size), :] - dot3(left, (high[SEP:, :], low[SEP:, :]))
        return child, 0

    assemble(table, place[1], place[2], update_rows, sep, upd, *outs)


def factor(place, pivot, below, rest, sep_count, upd_count, level, following):
    count = below.shape[0]
    total = SEP + count
    out_shape = [
        jax.ShapeDtypeStruct((sep_count, SEP), jnp.float32),
        jax.ShapeDtypeStruct((upd_count, SEP), jnp.float32),
    ]
    operands = [place, pivot, below]
    specs = [SCALARS, WHOLE, WHOLE]
    scratch = [
        pltpu.VMEM((SEP, SEP), jnp.float32),
        pltpu.VMEM((count, SEP), jnp.float32),
        pltpu.VMEM((total, TILE), jnp.float32),
        pltpu.VMEM((TILE, TILE), jnp.float32),
        pltpu.VMEM((total, SEP), jnp.bfloat16),
        pltpu.VMEM((total, SEP), jnp.bfloat16),
    ]
    if rest is not None:
        table, sep, upd = following
        out_shape += assembled_shapes(sep, upd, level + 1)
        operands += [rest, table, sep, upd]
        specs += [WHOLE, SCALARS, WHOLE, WHOLE]
        scratch.append(pltpu.VMEM((upd.shape[0], UPD), jnp.float32))
    return pl.pallas_call(
        functools.partial(factor_kernel, rest is not None),
        out_shape=tuple(out_shape),
        in_specs=specs,
        out_specs=(WHOLE,) * len(out_shape),
        scratch_shapes=scratch,
        compiler_params=pltpu.CompilerParams(vmem_limit_bytes=48 * 2**20),
    )(*operands)


def bit_of(index, bit):
    return lax.rem(lax.div(index, jnp.int32(2**bit)), jnp.int32(2))


def front_dims(level, front_bits):
    return [("leaf", bit) for bit in range(level - 1, -1, -1)] + [("front", bit) for bit in range(front_bits - 1, -1, -1)]


def orders_of(level, front_bits):
    links = list(range(level + front_bits - 1))
    last = level + front_bits - 1
    if level == 3:
        swapped = links[:-2] + [links[-1], links[-2]]
        return [links + [last], swapped + [last]]
    return [links[turn:] + links[:turn] + [last] for turn in range(len(links))]


def column_parts(columns, parts):
    tiles = columns // TILE
    cuts = [round(tiles * part / parts) * TILE for part in range(parts + 1)]
    return [(cuts[part], cuts[part + 1] - cuts[part]) for part in range(parts)]


def partner_of(dim):
    axis, bit = dim
    index = lax.axis_index(axis)
    return {axis: index + (1 - 2 * bit_of(index, bit)) * 2**bit}


def doubling(buffer, dims, order, columns, send, recv):
    bits = [bit_of(lax.axis_index(axis), bit) for axis, bit in dims]
    copies = []
    for step, dim in enumerate(order):
        index = tuple(slice(None) if d in order[:step] else bits[d] for d in range(len(dims)))
        part = buffer.at[index + (slice(None), pl.ds(*columns))]
        copies.append(pltpu.make_async_remote_copy(
            src_ref=part,
            dst_ref=part,
            send_sem=send.at[step],
            recv_sem=recv.at[step],
            device_id=partner_of(dims[dim]),
            device_id_type=MESH,
        ))
    return copies


def exchange_kernel(level, front_bits, own_sep, own_upd, out_sep, out_upd, *refs):
    last = level == 3
    if last:
        f11, below = refs[:2]
        buffers = [f11]
        refs = refs[2:]
    else:
        f11, f21, f22 = refs[:3]
        buffers = [f11, f21, f22]
        refs = refs[3:]
    recv_sep, recv_upd, own_send, own_recv, all_send, all_recv = refs
    dims = front_dims(level, front_bits)
    bits = [bit_of(lax.axis_index(axis), bit) for axis, bit in dims]

    barrier = pltpu.get_barrier_semaphore()
    for dim in dims:
        pl.semaphore_signal(barrier, inc=1, device_id=partner_of(dim), device_id_type=MESH)
    pl.semaphore_wait(barrier, len(dims))

    def to_sibling(src, dst, slot):
        return pltpu.make_async_remote_copy(
            src_ref=src, dst_ref=dst, send_sem=own_send.at[slot], recv_sem=own_recv.at[slot],
            device_id=partner_of(dims[0]), device_id_type=MESH)

    sep_copy = to_sibling(out_sep, recv_sep, 0)
    upd_copy = to_sibling(out_upd, recv_upd, 1)
    sep_copy.start()
    upd_copy.start()

    chains = []
    for item, buffer in enumerate(buffers):
        orders = orders_of(level, front_bits)
        for part, columns in enumerate(column_parts(buffer.shape[-1], len(orders))):
            slot = item * len(orders) + part
            chains.append(doubling(buffer, dims, orders[part], columns, all_send.at[slot], all_recv.at[slot]))
    first = len(orders)
    own = tuple(bits)

    sep_copy.wait()
    f11[own] = own_sep[...] + recv_sep[...]
    for chain in chains[:first]:
        chain[0].start()
    upd_copy.wait()
    if last:
        below[...] = own_upd[...] + recv_upd[...]
    else:
        f21[own] = own_upd[:, :SEP] + recv_upd[:, :SEP]
        f22[own] = own_upd[:, SEP:] + recv_upd[:, SEP:]
    for chain in chains[first:]:
        chain[0].start()
    for step in range(len(dims)):
        for chain in chains:
            chain[step].wait()
            if step + 1 < len(dims):
                chain[step + 1].start()


def exchange(level, front_bits, own_sep, own_upd, out_sep, out_upd):
    last = level == 3
    sep_count, upd_count = own_sep.shape[0], own_upd.shape[0]
    lead = (2,) * (level + front_bits)
    width = SEP if last else NF
    shapes = [lead + (sep_count, SEP)]
    shapes += [(upd_count, SEP)] if last else [lead + (upd_count, SEP), lead + (upd_count, UPD)]
    chains = len(orders_of(level, front_bits)) * (1 if last else 3)
    steps = len(lead)
    return pl.pallas_call(
        functools.partial(exchange_kernel, level, front_bits),
        out_shape=tuple(jax.ShapeDtypeStruct(shape, jnp.float32) for shape in shapes),
        in_specs=[WHOLE] * 4,
        out_specs=(WHOLE,) * len(shapes),
        scratch_shapes=[
            pltpu.VMEM((sep_count, SEP), jnp.float32),
            pltpu.VMEM((upd_count, width), jnp.float32),
            pltpu.SemaphoreType.DMA((2,)),
            pltpu.SemaphoreType.DMA((2,)),
            pltpu.SemaphoreType.DMA((chains, steps)),
            pltpu.SemaphoreType.DMA((chains, steps)),
        ],
        compiler_params=pltpu.CompilerParams(
            collective_id=level, has_side_effects=True, vmem_limit_bytes=48 * 2**20),
    )(own_sep, own_upd, out_sep, out_upd)


def tile_table(tile_map):
    tiles = jnp.arange(NT, dtype=jnp.int32)
    match = tile_map[:, None] == tiles[None, :]
    place = jnp.sum(jnp.where(match, jnp.arange(UT, dtype=jnp.int32)[:, None], 0), axis=0)
    return jnp.concatenate([place, jnp.any(match, axis=0).astype(jnp.int32)])


def body(
    leaf_update,
    separator_rows_1,
    remaining_rows_1,
    separator_rows_2,
    remaining_rows_2,
    separator_rows_3,
    remaining_rows_3,
    child_map_1,
    child_map_2,
    child_map_3,
):
    leaf_place = lax.axis_index("leaf")
    front_place = lax.axis_index("front")
    front_count = lax.axis_size("front")
    front_bits = front_count.bit_length() - 1
    sections = (
        (separator_rows_1, remaining_rows_1, child_map_1),
        (separator_rows_2, remaining_rows_2, child_map_2),
        (separator_rows_3, remaining_rows_3, child_map_3),
    )
    tables = [
        tile_table(lax.dynamic_index_in_dim(maps, leaf_place >> number, 0, keepdims=False))
        for number, (_, _, maps) in enumerate(sections)
    ]
    positions = [
        (leaf_place % 2**level * front_count + front_place, (leaf_place ^ 1 << level - 1) % 2**level * front_count + front_place)
        for level in range(1, 4)
    ]
    results = []
    sep, upd, _ = sections[0]
    rows = assemble_leaf(jnp.stack(positions[0]).astype(jnp.int32), tables[0], leaf_update, sep, upd)
    for level in range(1, 4):
        sep, upd, _ = sections[level - 1]
        parts = exchange(level, front_bits, *rows)
        pivot = parts[0].reshape(SEP, SEP)
        place = [positions[level - 1][0]]
        following = None
        if level < 3:
            below, rest = parts[1].reshape(UPD, SEP), parts[2].reshape(UPD, UPD)
            following = (tables[level],) + sections[level][:2]
            place += positions[level]
        else:
            below, rest = parts[1], None
        place = jnp.stack(place).astype(jnp.int32)
        outs = factor(place, pivot, below, rest, sep.shape[0], upd.shape[0], level, following)
        results += outs[:2]
        rows = outs[2:]
    return tuple(results)


def solution(mesh):
    rows = P(("leaf", "front"), None)
    in_specs = (P("leaf", None),) + (rows,) * 6 + (P(),) * 3
    return jax.shard_map(body, mesh=mesh, in_specs=in_specs, out_specs=(rows,) * 6, check_vma=False)
```

time: 858 us -> 234 us (0.27)
  other arithmetic: 380 us -> 0.83 us
  waiting for transfers between devices: 280 us -> 0 us
  Pallas kernels: 88.3 us -> 226 us
  local copies, waits for them, and re-layouts: 51 us -> 5.72 us
  starting transfers between devices: 19 us -> 0 us
  between operations: 15 us -> 0.84 us
  blocking collectives: 13.1 us -> 0 us
    unnamed x66 -> x0, other arithmetic: 331 us -> none
    ppermute x12 -> x0, waiting for transfers between devices: 221 us -> none  [from_partner(): return lax.ppermute(block, axis, route)]
    pallas_call x3 -> x7, Pallas kernels: 88.3 us -> 226 us  [the longest x3 128 us: exchange(): pl.pallas_call(functools.partial(exchange_kernel, level, front_bits), out...]
    all_gather x3 -> x0, waiting for transfers between devices: 59.1 us -> none  [collect(): gathered = lax.all_gather(pieces, 'front', axis=0, tiled=True)]
    concatenate x6 -> x2, other arithmetic: 30 us -> 0.15 us  [tile_table(): return jnp.concatenate([place, jnp.any(match, axis=0).astype(jnp.int32)])]
    slice x44 -> x0, local copies, waits for them, and re-layouts: 29.2 us -> none  [the longest x36 25.1 us: expand_columns(): placing[u, n]]
    gather x6 -> x0, local copies, waits for them, and re-layouts: 19 us -> none  [select_rows(): jnp.take(full_update, source, axis=0)]
    ppermute x12 -> x0, starting transfers between devices: 18.5 us -> none  [from_partner(): return lax.ppermute(block, axis, route)]
  transfers between devices with their start and end apart: 15 -> 0, of which waited for: 12 -> 0; matrix products, arithmetic and copies ran while one was open for 25% -> 0% of each run, Pallas kernels for 0% -> 0%
where the time goes in v2:
time: 234 us; the launch traced here: 233 us
  Pallas kernels  226 us (97%)
  local copies, waits for them, and re-layouts  5.72 us (2%)
    pallas_call x3, Pallas kernels, exchange(): pl.pallas_call(functools.partial(exchange_kernel, level, front_bits), out...  128 us
    pallas_call x3, Pallas kernels, factor(): pl.pallas_call(functools.partial(factor_kernel, rest is not None), out_sh...  97.3 us

profile of v2, /device:TPU:0, one launch (start us, length us, event | category | flops | bytes accessed | tf_op | source)
XLA Modules:
  0.0 233.4 jit_solution(10268689233554448488)
XLA Ops:
  0.6 0.0 copy-start
  0.6 0.0 copy-start.5
  0.8 0.1 pad_add_fusion
  0.8 0.1 pad_add_fusion.1.place
  0.9 0.7 fusion.5
  1.6 0.7 fusion.4
  2.3 0.0 copy-done
  2.3 0.1 fusion.2
  2.4 0.1 select_reduce_fusion.2
  2.5 0.1 fusion.1
  2.5 0.1 select_reduce_fusion.1
  2.6 0.1 pad_add_fusion.2
  2.7 0.1 fusion
  2.8 0.1 select_reduce_fusion
  2.9 0.1 pad_add_fusion.5.refs_1_
  3.0 0.0 copy-start.1
  3.0 2.2 copy-done.1
  5.2 0.0 copy-start.2
  5.2 1.1 copy-done.2
  6.3 0.0 copy-start.4
  6.3 1.0 copy-done.4
  7.3 0.0 copy-start.3
  7.3 0.8 shard_map.145
  8.1 60.1 %shard_map.146 = (f32[2,2,2,64,512]{4,3,2,1,0:T(8,128)S(1)}, f32[2,2,2,128,512]{4,3,2,1,0:T(8,128)S(1)}, f32[2,2,2,128,1024]{4,3,2,1,0:T(8,128)}) custom-call(f32[64,512]{1,0:T(8,128)S(1)} %get-tuple-element.32.own_sep, f32[128,1536]{1,0:T(8,128)S(1)} %get-tuple-element.33.own_upd, f32[64,512]{1,0:T(8,128)S(1)} %get-tuple-element.34.out_sep, ...), custom_call_target="tpu_custom_call" | custom-call | tf_op jit(solution)/shard_map/pallas_call | solution.py:324
  68.2 0.0 copy-done.5
  68.3 0.0 copy-done.3
  68.3 0.0 copy-start.6
  68.3 0.0 copy-start.7
  68.3 36.5 %shard_map.147 = (f32[64,512]{1,0:T(8,128)}, f32[128,512]{1,0:T(8,128)}, f32[32,512]{1,0:T(8,128)S(1)}, f32[64,1536]{1,0:T(8,128)S(1)}, f32[32,512]{1,0:T(8,128)S(1)}, /*index=5*/f32[64,1536]{1,0:T(8,128)S(1)}) custom-call(s32[3]{0:T(128)S(1)} %get-tuple-element.58.place, f32[512,512]{1,0:T(8,128)S(1)} %bitcast.21, f32[1024,512]{1,0:T(8,128)S(1)} %bitcast.19, ...), custom_call_target="tpu_custom_call" | custom-call | tf_op jit(solution)/shard_map/pallas_call | solution.py:202
  104.8 43.6 %shard_map.148 = (f32[2,2,2,2,32,512]{5,4,3,2,1,0:T(8,128)S(1)}, f32[2,2,2,2,64,512]{5,4,3,2,1,0:T(8,128)S(1)}, f32[2,2,2,2,64,1024]{5,4,3,2,1,0:T(8,128)}) custom-call(f32[32,512]{1,0:T(8,128)S(1)} %get-tuple-element.41.own_sep, f32[64,1536]{1,0:T(8,128)S(1)} %get-tuple-element.42.own_upd, f32[32,512]{1,0:T(8,128)S(1)} %get-tuple-element.43.out_sep, ...), custom_call_target="tpu_custom_call" | custom-call | tf_op jit(solution)/shard_map/pallas_call | solution.py:324
  148.4 0.0 copy-done.6
  148.5 0.0 copy-done.7
  148.5 36.2 %shard_map.149 = (f32[32,512]{1,0:T(8,128)}, f32[64,512]{1,0:T(8,128)}, f32[16,512]{1,0:T(8,128)S(1)}, f32[32,512]{1,0:T(8,128)S(1)}, f32[16,512]{1,0:T(8,128)S(1)}, /*index=5*/f32[32,512]{1,0:T(8,128)S(1)}) custom-call(s32[3]{0:T(128)S(1)} %get-tuple-element.59.place, f32[512,512]{1,0:T(8,128)S(1)} %bitcast.23, f32[1024,512]{1,0:T(8,128)S(1)} %bitcast.20, ...), custom_call_target="tpu_custom_call" | custom-call | tf_op jit(solution)/shard_map/pallas_call | solution.py:202
  184.7 24.1 %shard_map.150 = (f32[2,2,2,2,2,16,512]{6,5,4,3,2,1,0:T(8,128)S(1)}, f32[32,512]{1,0:T(8,128)S(1)}) custom-call(f32[16,512]{1,0:T(8,128)S(1)} %get-tuple-element.50.own_sep, f32[32,512]{1,0:T(8,128)S(1)} %get-tuple-element.51.own_upd, f32[16,512]{1,0:T(8,128)S(1)} %get-tuple-element.52.out_sep, f32[32,512]{1,0:T(8,128)S(1)} %get-tuple-element.53.out_upd), custom_call_target="tpu_custom_call" | custom-call | tf_op jit(solution)/shard_map/pallas_call | solution.py:324
  208.8 24.6 %shard_map.151 = (f32[16,512]{1,0:T(8,128)}, f32[32,512]{1,0:T(8,128)}) custom-call(s32[1]{0:T(128)} %bitcast.9.place, f32[512,512]{1,0:T(8,128)S(1)} %bitcast.22, f32[32,512]{1,0:T(8,128)S(1)} %get-tuple-element.55.below), custom_call_target="tpu_custom_call" | custom-call | tf_op jit(solution)/shard_map/pallas_call | solution.py:202
  (4 shorter events, 0.0 us)
Async XLA Ops:
  0.6 1.6 copy-start
  0.6 67.6 %copy-start.5 = (f32[32,1536]{1,0:T(8,128)S(1)}, f32[32,1536]{1,0:T(8,128)}, u32[]{:S(2)}) copy-start(f32[32,1536]{1,0:T(8,128)} %refs_2_.2) | copy-start | bytes 589828
  3.0 2.2 copy-start.1
  5.2 1.1 copy-start.2
  6.3 1.0 copy-start.4
  7.3 61.0 %copy-start.3 = (f32[64,1536]{1,0:T(8,128)S(1)}, f32[64,1536]{1,0:T(8,128)}, u32[]{:S(2)}) copy-start(f32[64,1536]{1,0:T(8,128)} %refs_3_.2) | copy-start | bytes 1179652
  68.3 80.2 %copy-start.6 = (f32[32,1536]{1,0:T(8,128)S(1)}, f32[32,1536]{1,0:T(8,128)}, u32[]{:S(2)}) copy-start(f32[32,1536]{1,0:T(8,128)} %refs_3_.3) | copy-start | bytes 589828
  68.3 80.2 %copy-start.7 = (f32[16,1536]{1,0:T(8,128)S(1)}, f32[16,1536]{1,0:T(8,128)}, u32[]{:S(2)}) copy-start(f32[16,1536]{1,0:T(8,128)} %refs_2_.3) | copy-start | bytes 294916

commit v3 on v2

--- a/solution.py
+++ b/solution.py
@@ -45,16 +45,22 @@
         aug = jnp.where(in_strip, jnp.where(lane - base == sub, 1.0, 0.0), strip)
         x = [jnp.broadcast_to(aug[i:i + 1, :], full) for i in range(STRIP)]
         r = []
-        for k in range(STRIP):
+        for k in range(0, STRIP, 2):
+            n = k + 1
+            det = d[k, k] * d[n, n] - d[n, k] * d[n, k]
             r.append(lax.rsqrt(d[k, k]))
-            for i in range(k + 1, STRIP):
+            r.append(d[k, k] * r[k] * lax.rsqrt(det))
+            d[n, k] = d[n, k] * r[k]
+            for i in range(k + 2, STRIP):
                 d[i, k] = d[i, k] * r[k]
-            for j in range(k + 1, STRIP):
+                d[i, n] = (d[i, n] - d[i, k] * d[n, k]) * r[n]
+            for j in range(k + 2, STRIP):
                 for i in range(j, STRIP):
-                    d[i, j] = d[i, j] - d[i, k] * d[j, k]
+                    d[i, j] = d[i, j] - (d[i, k] * d[j, k] + d[i, n] * d[j, n])
             x[k] = x[k] * r[k]
-            for i in range(k + 1, STRIP):
-                x[i] = x[i] - d[i, k] * x[k]
+            x[n] = (x[n] - d[n, k] * x[k]) * r[n]
+            for i in range(k + 2, STRIP):
+                x[i] = x[i] - (d[i, k] * x[k] + d[i, n] * x[n])
         u = x[0]
         for k in range(1, STRIP):
             u = jnp.where(sub == k, x[k], u)
@@ -75,24 +81,27 @@
     return out
 
 
-def factor_block(b, pivot, below, work, inv, high, low):
-    total = work.shape[0]
+def pivot_block(b, pivot, diag, work, inv, high, low):
     start = pl.multiple_of(b * TILE, TILE)
     here = pl.ds(start, TILE)
-    done = dot3((high[...], low[...]), (high[here, :], low[here, :]))
-    work[:SEP, :] = pivot[:, here] - done[:SEP]
-    work[SEP:, :] = below[:, here] - done[SEP:]
+    work[...] = pivot(here) - dot3((high[...], low[...]), (high[here, :], low[here, :]))
     strips = [work[pl.ds(pl.multiple_of(start + STRIP * t, STRIP), STRIP), :] for t in range(TILE // STRIP)]
     for t, strip in enumerate(invert_block(strips)):
-        inv[STRIP * t:STRIP * t + STRIP, :] = strip
-    column = dot3(split(work[...]), split(inv[...]))
-    row_ids = lax.broadcasted_iota(jnp.int32, (total, TILE), 0)
-    col_ids = lax.broadcasted_iota(jnp.int32, (total, TILE), 1) + start
+        inv[b, STRIP * t:STRIP * t + STRIP, :] = strip
+    column = dot3(split(work[...]), split(inv[b]))
+    row_ids = lax.broadcasted_iota(jnp.int32, (SEP, TILE), 0)
+    col_ids = lax.broadcasted_iota(jnp.int32, (SEP, TILE), 1) + start
     column = jnp.where(row_ids >= col_ids, column, 0.0)
-    high_part, low_part = split(column)
-    high[:, here] = high_part
-    low[:, here] = low_part
-    return column
+    diag[:, here] = column
+    high[:, here], low[:, here] = split(column)
+
+
+def solve_block(b, below, solved, inv, high, low, done_high, done_low):
+    here = pl.ds(pl.multiple_of(b * TILE, TILE), TILE)
+    rest = below(here) - dot3((done_high[...], done_low[...]), (high[here, :], low[here, :]))
+    column = dot3(split(rest), split(inv[b]))
+    solved[:, here] = column
+    done_high[:, here], done_low[:, here] = split(column)
 
 
 def child_piece(table, row, count):
@@ -143,70 +152,32 @@
     )(place, table, leaf, sep, upd)
 
 
-def factor_kernel(with_update, place, pivot, below, *refs):
-    if with_update:
-        rest, table, sep, upd, diag, solved, *outs = refs
-        outs, refs = outs[:4], outs[4:]
-        full_diag, full_solved, work, inv, high, low, child = refs
-    else:
-        diag, solved, full_diag, full_solved, work, inv, high, low = refs
-    high[...] = jnp.zeros_like(high)
-    low[...] = jnp.zeros_like(low)
-
-    @pl.loop(0, SEP // TILE)
-    def _(b):
-        column = factor_block(b, pivot, below, work, inv, high, low)
-        here = pl.ds(pl.multiple_of(b * TILE, TILE), TILE)
-        full_diag[:, here] = column[:SEP]
-        full_solved[:, here] = column[SEP:]
-
-    sep_count = diag.shape[0]
-    diag[...] = full_diag[pl.ds(pl.multiple_of(place[0] * sep_count, 8), sep_count), :]
-    if not with_update:
-        solved[...] = full_solved[...]
-        return
-    upd_count = solved.shape[0]
-    solved[...] = full_solved[pl.ds(pl.multiple_of(place[0] * upd_count, 8), upd_count), :]
+def update_kernel(place, table, solved, rest, sep, upd, *refs):
+    outs, (high, low, child) = refs[:4], refs[4:]
+    high[...], low[...] = split(solved[...])
 
     def update_rows(here, size):
-        left = split(full_solved[pl.ds(here, size), :])
-        child[:size, :] = rest[pl.ds(here, size), :] - dot3(left, (high[SEP:, :], low[SEP:, :]))
+        left = split(solved[pl.ds(here, size), :])
+        child[:size, :] = rest[pl.ds(here, size), :] - dot3(left, (high[...], low[...]))
         return child, 0
 
-    assemble(table, place[1], place[2], update_rows, sep, upd, *outs)
-
-
-def factor(place, pivot, below, rest, sep_count, upd_count, level, following):
-    count = below.shape[0]
-    total = SEP + count
-    out_shape = [
-        jax.ShapeDtypeStruct((sep_count, SEP), jnp.float32),
-        jax.ShapeDtypeStruct((upd_count, SEP), jnp.float32),
-    ]
-    operands = [place, pivot, below]
-    specs = [SCALARS, WHOLE, WHOLE]
-    scratch = [
-        pltpu.VMEM((SEP, SEP), jnp.float32),
-        pltpu.VMEM((count, SEP), jnp.float32),
-        pltpu.VMEM((total, TILE), jnp.float32),
-        pltpu.VMEM((TILE, TILE), jnp.float32),
-        pltpu.VMEM((total, SEP), jnp.bfloat16),
-        pltpu.VMEM((total, SEP), jnp.bfloat16),
-    ]
-    if rest is not None:
-        table, sep, upd = following
-        out_shape += assembled_shapes(sep, upd, level + 1)
-        operands += [rest, table, sep, upd]
-        specs += [WHOLE, SCALARS, WHOLE, WHOLE]
-        scratch.append(pltpu.VMEM((upd.shape[0], UPD), jnp.float32))
+    assemble(table, place[0], place[1], update_rows, sep, upd, *outs)
+
+
+def update(place, table, solved, rest, sep, upd, level):
+    shapes = assembled_shapes(sep, upd, level)
     return pl.pallas_call(
-        functools.partial(factor_kernel, rest is not None),
-        out_shape=tuple(out_shape),
-        in_specs=specs,
-        out_specs=(WHOLE,) * len(out_shape),
-        scratch_shapes=scratch,
-        compiler_params=pltpu.CompilerParams(vmem_limit_bytes=48 * 2**20),
-    )(*operands)
+        update_kernel,
+        out_shape=tuple(shapes),
+        in_specs=[SCALARS] * 2 + [WHOLE] * 4,
+        out_specs=(WHOLE,) * 4,
+        scratch_shapes=[
+            pltpu.VMEM((UPD, SEP), jnp.bfloat16),
+            pltpu.VMEM((UPD, SEP), jnp.bfloat16),
+            pltpu.VMEM((upd.shape[0], UPD), jnp.float32),
+        ],
+        compiler_params=pltpu.CompilerParams(vmem_limit_bytes=40 * 2**20),
+    )(place, table, solved, rest, sep, upd)
 
 
 def bit_of(index, bit):
@@ -255,24 +226,24 @@
     return copies
 
 
-def exchange_kernel(level, front_bits, own_sep, own_upd, out_sep, out_upd, *refs):
+def level_kernel(level, front_bits, own_sep, own_upd, out_sep, out_upd, *refs):
     last = level == 3
     if last:
-        f11, below = refs[:2]
-        buffers = [f11]
-        refs = refs[2:]
+        diag, solved, below, full_solved, *refs = refs
     else:
-        f11, f21, f22 = refs[:3]
-        buffers = [f11, f21, f22]
-        refs = refs[3:]
+        diag, solved, full_solved, f22, f21, *refs = refs
+    f11, full_diag, work, inv, high, low, done_high, done_low, *refs = refs
     recv_sep, recv_upd, own_send, own_recv, all_send, all_recv = refs
+    buffers = [f11] if last else [f11, f21, f22]
     dims = front_dims(level, front_bits)
     bits = [bit_of(lax.axis_index(axis), bit) for axis, bit in dims]
+    steps = len(dims)
+    position = lax.rem(lax.axis_index("leaf"), jnp.int32(2**level)) * 2**front_bits + lax.axis_index("front")
 
     barrier = pltpu.get_barrier_semaphore()
     for dim in dims:
         pl.semaphore_signal(barrier, inc=1, device_id=partner_of(dim), device_id_type=MESH)
-    pl.semaphore_wait(barrier, len(dims))
+    pl.semaphore_wait(barrier, steps)
 
     def to_sibling(src, dst, slot):
         return pltpu.make_async_remote_copy(
@@ -282,53 +253,105 @@
     sep_copy = to_sibling(out_sep, recv_sep, 0)
     upd_copy = to_sibling(out_upd, recv_upd, 1)
     sep_copy.start()
-    upd_copy.start()
+    high[...] = jnp.zeros_like(high)
+    low[...] = jnp.zeros_like(low)
+    done_high[...] = jnp.zeros_like(done_high)
+    done_low[...] = jnp.zeros_like(done_low)
 
     chains = []
+    orders = orders_of(level, front_bits)
     for item, buffer in enumerate(buffers):
-        orders = orders_of(level, front_bits)
         for part, columns in enumerate(column_parts(buffer.shape[-1], len(orders))):
             slot = item * len(orders) + part
             chains.append(doubling(buffer, dims, orders[part], columns, all_send.at[slot], all_recv.at[slot]))
-    first = len(orders)
+    early, late = chains[:len(orders)], chains[len(orders):]
     own = tuple(bits)
+
+    def advance(which, step):
+        for chain in which:
+            if step >= 0:
+                chain[step].wait()
+            if step + 1 < steps:
+                chain[step + 1].start()
 
     sep_copy.wait()
     f11[own] = own_sep[...] + recv_sep[...]
-    for chain in chains[:first]:
-        chain[0].start()
-    upd_copy.wait()
+    advance(early, -1)
+    for step in range(steps):
+        if step == steps - 1:
+            upd_copy.start()
+        advance(early, step)
+
+    def arrived():
+        upd_copy.wait()
+        if last:
+            below[...] = own_upd[...] + recv_upd[...]
+        else:
+            f21[own] = own_upd[:, :SEP] + recv_upd[:, :SEP]
+            f22[own] = own_upd[:, SEP:] + recv_upd[:, SEP:]
+            advance(late, -1)
+
+    blocks = SEP // TILE
+    flat = (slice(None),) * len(dims)
+
+    @pl.loop(0, blocks)
+    def _(b):
+        pivot_block(b, lambda here: f11[flat + (slice(None), here)].reshape(SEP, TILE), full_diag, work, inv, high, low)
+
+        @pl.when(b == 0)
+        def _():
+            arrived()
+
+        if not last:
+            for step in range(steps - 1):
+                @pl.when(b == blocks - steps + 1 + step)
+                def _():
+                    advance(late, step)
+
+    for chain in late[:len(orders)]:
+        chain[steps - 1].wait()
+
+    @pl.loop(0, blocks)
+    def _(b):
+        if last:
+            piece = lambda here: below[:, here]
+        else:
+            piece = lambda here: f21[flat + (slice(None), here)].reshape(UPD, TILE)
+        solve_block(b, piece, full_solved, inv, high, low, done_high, done_low)
+
+    sep_count, upd_count = diag.shape[0], solved.shape[0]
+    diag[...] = full_diag[pl.ds(pl.multiple_of(position * sep_count, 8), sep_count), :]
     if last:
-        below[...] = own_upd[...] + recv_upd[...]
+        solved[...] = full_solved[...]
     else:
-        f21[own] = own_upd[:, :SEP] + recv_upd[:, :SEP]
-        f22[own] = own_upd[:, SEP:] + recv_upd[:, SEP:]
-    for chain in chains[first:]:
-        chain[0].start()
-    for step in range(len(dims)):
-        for chain in chains:
-            chain[step].wait()
-            if step + 1 < len(dims):
-                chain[step + 1].start()
-
-
-def exchange(level, front_bits, own_sep, own_upd, out_sep, out_upd):
+        solved[...] = full_solved[pl.ds(pl.multiple_of(position * upd_count, 8), upd_count), :]
+    for chain in late[len(orders):]:
+        chain[steps - 1].wait()
+
+
+def factor_level(level, front_bits, own_sep, own_upd, out_sep, out_upd):
     last = level == 3
     sep_count, upd_count = own_sep.shape[0], own_upd.shape[0]
     lead = (2,) * (level + front_bits)
-    width = SEP if last else NF
-    shapes = [lead + (sep_count, SEP)]
-    shapes += [(upd_count, SEP)] if last else [lead + (upd_count, SEP), lead + (upd_count, UPD)]
+    steps = len(lead)
+    rows = upd_count if last else UPD
+    shapes = [(sep_count, SEP), (upd_count, SEP)]
+    scratch = [(upd_count, SEP), (upd_count, SEP)] if last else [lead + (upd_count, SEP)]
+    if not last:
+        shapes += [(UPD, SEP), lead + (upd_count, UPD)]
+    scratch += [lead + (sep_count, SEP), (SEP, SEP), (SEP, TILE), (SEP // TILE, TILE, TILE)]
+    halves = [(SEP, SEP)] * 2 + [(rows, SEP)] * 2
+    received = [own_sep.shape, own_upd.shape]
     chains = len(orders_of(level, front_bits)) * (1 if last else 3)
-    steps = len(lead)
     return pl.pallas_call(
-        functools.partial(exchange_kernel, level, front_bits),
+        functools.partial(level_kernel, level, front_bits),
         out_shape=tuple(jax.ShapeDtypeStruct(shape, jnp.float32) for shape in shapes),
         in_specs=[WHOLE] * 4,
         out_specs=(WHOLE,) * len(shapes),
-        scratch_shapes=[
-            pltpu.VMEM((sep_count, SEP), jnp.float32),
-            pltpu.VMEM((upd_count, width), jnp.float32),
+        scratch_shapes=[pltpu.VMEM(shape, jnp.float32) for shape in scratch]
+        + [pltpu.VMEM(shape, jnp.bfloat16) for shape in halves]
+        + [pltpu.VMEM(shape, jnp.float32) for shape in received]
+        + [
             pltpu.SemaphoreType.DMA((2,)),
             pltpu.SemaphoreType.DMA((2,)),
             pltpu.SemaphoreType.DMA((chains, steps)),
@@ -379,21 +402,12 @@
     sep, upd, _ = sections[0]
     rows = assemble_leaf(jnp.stack(positions[0]).astype(jnp.int32), tables[0], leaf_update, sep, upd)
     for level in range(1, 4):
-        sep, upd, _ = sections[level - 1]
-        parts = exchange(level, front_bits, *rows)
-        pivot = parts[0].reshape(SEP, SEP)
-        place = [positions[level - 1][0]]
-        following = None
+        outs = factor_level(level, front_bits, *rows)
+        results += outs[:2]
         if level < 3:
-            below, rest = parts[1].reshape(UPD, SEP), parts[2].reshape(UPD, UPD)
-            following = (tables[level],) + sections[level][:2]
-            place += positions[level]
-        else:
-            below, rest = parts[1], None
-        place = jnp.stack(place).astype(jnp.int32)
-        outs = factor(place, pivot, below, rest, sep.shape[0], upd.shape[0], level, following)
-        results += outs[:2]
-        rows = outs[2:]
+            place = jnp.stack(positions[level]).astype(jnp.int32)
+            sep, upd, _ = sections[level]
+            rows = update(place, tables[level], outs[2], outs[3].reshape(UPD, UPD), sep, upd, level + 1)
     return tuple(results)
 
 

time: 234 us -> 198 us (0.85)
  Pallas kernels: 226 us -> 181 us
  local copies, waits for them, and re-layouts: 5.72 us -> 14 us
    pallas_call x6 -> x5, Pallas kernels: 225 us -> 181 us  [the longest x3 172 us: factor_level(): pl.pallas_call(functools.partial(level_kernel, level, front_bits), out_sh...]
    unnamed x16 -> x26, local copies, waits for them, and re-layouts: 4.35 us -> 12.6 us
where the time goes in v3:
time: 198 us; the launch traced here: 197 us
  Pallas kernels  181 us (91%)
  local copies, waits for them, and re-layouts  14 us (7%)
    pallas_call x3, Pallas kernels, factor_level(): pl.pallas_call(functools.partial(level_kernel, level, front_bits), out_sh...  172 us
    unnamed x26, local copies, waits for them, and re-layouts  12.6 us
    pallas_call x2, Pallas kernels, update(): pl.pallas_call(update_kernel, out_shape=tuple(shapes), in_specs=[SCALARS]...  8.57 us

profile of v3, /device:TPU:0, one launch (start us, length us, event | category | flops | bytes accessed | tf_op | source)
XLA Modules:
  0.0 197.2 jit_solution(445696743975052289)
XLA Ops:
  0.6 0.0 copy-start
  0.6 0.0 copy-start.7
  0.7 0.1 pad_add_fusion
  0.8 0.1 pad_add_fusion.4.place
  0.9 0.7 fusion.5
  1.6 0.7 fusion.4
  2.3 0.0 copy-done
  2.3 0.1 fusion.2
  2.4 0.1 select_reduce_fusion.2
  2.5 0.1 fusion.1
  2.5 0.1 select_reduce_fusion.1
  2.6 0.1 pad_add_fusion.1
  2.7 0.1 fusion
  2.8 0.1 select_reduce_fusion
  2.9 0.1 pad_add_fusion.5.table
  3.0 0.0 copy-start.1
  3.0 2.2 %copy-done.1 = f32[1024,1024]{1,0:T(8,128)S(1)} copy-done((f32[1024,1024]{1,0:T(8,128)S(1)}, f32[1024,1024]{1,0:T(8,128)}, u32[]{:S(2)}) %copy-start.1) | copy-done | bytes 4194328
  5.2 0.0 copy-start.4
  5.2 1.1 copy-done.4
  6.3 0.0 copy-start.5
  6.3 1.0 copy-done.5
  7.3 0.0 copy-start.6
  7.3 0.8 shard_map.145
  8.1 0.0 copy-start.8
  8.1 0.0 copy-start.9
  8.2 67.8 %shard_map.146 = (f32[64,512]{1,0:T(8,128)S(1)}, f32[128,512]{1,0:T(8,128)S(1)}, f32[1024,512]{1,0:T(8,128)S(1)}, f32[2,2,2,128,1024]{4,3,2,1,0:T(8,128)}) custom-call(f32[64,512]{1,0:T(8,128)S(1)} %get-tuple-element.28.own_sep, f32[128,1536]{1,0:T(8,128)S(1)} %get-tuple-element.29.own_upd, f32[64,512]{1,0:T(8,128)S(1)} %get-tuple-element.30.out_sep, ...), custom_call_target="tpu_custom_call" | custom-call | tf_op jit(solution)/shard_map/pallas_call | solution.py:346
  76.0 0.0 copy-done.7
  76.0 0.0 copy-done.6
  76.0 0.0 copy-start.2
  76.0 2.2 %copy-done.2 = f32[2,2,2,128,1024]{4,3,2,1,0:T(8,128)S(1)} copy-done((f32[2,2,2,128,1024]{4,3,2,1,0:T(8,128)S(1)}, f32[2,2,2,128,1024]{4,3,2,1,0:T(8,128)}, u32[]{:S(2)}) %copy-start.2) | copy-done | bytes 4194328
  78.2 4.5 %shard_map.147 = (f32[32,512]{1,0:T(8,128)S(1)}, f32[64,1536]{1,0:T(8,128)S(1)}, f32[32,512]{1,0:T(8,128)S(1)}, f32[64,1536]{1,0:T(8,128)S(1)}) custom-call(s32[2]{0:T(128)S(1)} %get-tuple-element.51.place, s32[24]{0:T(128)S(1)} %get-tuple-element.53.table, f32[1024,512]{1,0:T(8,128)S(1)} %get-tuple-element.34.solved, f32[1024,1024]{1,0:T(8,128)S(1)} %bitcast.14, ...), custom_call_target="tpu_custom_call" | custom-call | tf_op jit(solution)/shard_map/pallas_call | solution.py:169
  82.7 58.4 %shard_map.148 = (f32[32,512]{1,0:T(8,128)S(1)}, f32[64,512]{1,0:T(8,128)S(1)}, f32[1024,512]{1,0:T(8,128)S(1)}, f32[2,2,2,2,64,1024]{5,4,3,2,1,0:T(8,128)}) custom-call(f32[32,512]{1,0:T(8,128)S(1)} %get-tuple-element.36.own_sep, f32[64,1536]{1,0:T(8,128)S(1)} %get-tuple-element.37.own_upd, f32[32,512]{1,0:T(8,128)S(1)} %get-tuple-element.38.out_sep, ...), custom_call_target="tpu_custom_call" | custom-call | tf_op jit(solution)/shard_map/pallas_call | solution.py:346
  141.1 0.0 copy-done.8
  141.1 0.0 copy-done.9
  141.1 0.0 copy-start.3
  141.1 2.2 %copy-done.3 = f32[2,2,2,2,64,1024]{5,4,3,2,1,0:T(8,128)S(1)} copy-done((f32[2,2,2,2,64,1024]{5,4,3,2,1,0:T(8,128)S(1)}, f32[2,2,2,2,64,1024]{5,4,3,2,1,0:T(8,128)}, u32[]{:S(2)}) %copy-start.3) | copy-done | bytes 4194328
  143.3 4.1 %shard_map.149 = (f32[16,512]{1,0:T(8,128)S(1)}, f32[32,512]{1,0:T(8,128)S(1)}, f32[16,512]{1,0:T(8,128)S(1)}, f32[32,512]{1,0:T(8,128)S(1)}) custom-call(s32[2]{0:T(128)S(1)} %pad_add_fusion.4.place, s32[24]{0:T(128)S(1)} %pad_add_fusion.5.table, f32[1024,512]{1,0:T(8,128)S(1)} %get-tuple-element.42.solved, f32[1024,1024]{1,0:T(8,128)S(1)} %bitcast.15, ...), custom_call_target="tpu_custom_call" | custom-call | tf_op jit(solution)/shard_map/pallas_call | solution.py:169
  147.4 45.9 %shard_map.150 = (f32[16,512]{1,0:T(8,128)S(1)}, f32[32,512]{1,0:T(8,128)S(1)}) custom-call(f32[16,512]{1,0:T(8,128)S(1)} %get-tuple-element.44.own_sep, f32[32,512]{1,0:T(8,128)S(1)} %get-tuple-element.45.own_upd, f32[16,512]{1,0:T(8,128)S(1)} %get-tuple-element.46.out_sep, f32[32,512]{1,0:T(8,128)S(1)} %get-tuple-element.47.out_upd), custom_call_target="tpu_custom_call" | custom-call | tf_op jit(solution)/shard_map/pallas_call | solution.py:346
  193.3 0.7 copy.22
  193.9 0.7 copy.23
  194.6 0.6 copy.24
  195.3 0.7 copy.25
  195.9 0.6 copy.26
  196.5 0.6 copy.27
  (4 shorter events, 0.0 us)
Async XLA Ops:
  0.6 1.6 copy-start
  0.6 75.3 %copy-start.7 = (f32[32,1536]{1,0:T(8,128)S(1)}, f32[32,1536]{1,0:T(8,128)}, u32[]{:S(2)}) copy-start(f32[32,1536]{1,0:T(8,128)} %sep.4) | copy-start | bytes 589828
  3.0 2.2 %copy-start.1 = (f32[1024,1024]{1,0:T(8,128)S(1)}, f32[1024,1024]{1,0:T(8,128)}, u32[]{:S(2)}) copy-start(f32[1024,1024]{1,0:T(8,128)} %leaf.1) | copy-start | bytes 12582916
  5.2 1.1 copy-start.4
  6.3 1.0 copy-start.5
  7.3 68.7 %copy-start.6 = (f32[64,1536]{1,0:T(8,128)S(1)}, f32[64,1536]{1,0:T(8,128)}, u32[]{:S(2)}) copy-start(f32[64,1536]{1,0:T(8,128)} %upd.4) | copy-start | bytes 1179652
  8.1 132.9 %copy-start.8 = (f32[32,1536]{1,0:T(8,128)S(1)}, f32[32,1536]{1,0:T(8,128)}, u32[]{:S(2)}) copy-start(f32[32,1536]{1,0:T(8,128)} %upd.5) | copy-start | bytes 589828
  8.1 132.9 %copy-start.9 = (f32[16,1536]{1,0:T(8,128)S(1)}, f32[16,1536]{1,0:T(8,128)}, u32[]{:S(2)}) copy-start(f32[16,1536]{1,0:T(8,128)} %sep.5) | copy-start | bytes 294916
  76.0 2.2 %copy-start.2 = (f32[2,2,2,128,1024]{4,3,2,1,0:T(8,128)S(1)}, f32[2,2,2,128,1024]{4,3,2,1,0:T(8,128)}, u32[]{:S(2)}) copy-start(f32[2,2,2,128,1024]{4,3,2,1,0:T(8,128)} %get-tuple-element.35) | copy-start | bytes 12582916
  141.1 2.2 %copy-start.3 = (f32[2,2,2,2,64,1024]{5,4,3,2,1,0:T(8,128)S(1)}, f32[2,2,2,2,64,1024]{5,4,3,2,1,0:T(8,128)}, u32[]{:S(2)}) copy-start(f32[2,2,2,2,64,1024]{5,4,3,2,1,0:T(8,128)} %get-tuple-element.43) | copy-start | bytes 12582916

commit v4 on v3

--- a/solution.py
+++ b/solution.py
@@ -115,23 +115,32 @@
     return rows[pl.ds(here, count), there] * (present * table[NT + n].astype(jnp.float32))
 
 
-def assemble(table, own, other, child_rows, sep, upd, own_sep, own_upd, out_sep, out_upd):
-    for out, size, offset, place, entries in (
+def assemble(table, own, other, child, finish, sep, upd, own_sep, own_upd, out_sep, out_upd, staged, sems):
+    plan = (
         (out_sep, sep.shape[0], 0, other, None),
         (own_sep, sep.shape[0], 0, own, sep),
         (out_upd, upd.shape[0], SEP, other, None),
         (own_upd, upd.shape[0], SEP, own, upd),
-    ):
+    )
+    pieces = []
+    for number, (out, size, offset, place, entries) in enumerate(plan):
         here, present = child_piece(table, offset + place * size, size)
-        rows, here = child_rows(here, size)
+        copy = pltpu.make_async_copy(child.at[pl.ds(here, size), :], staged.at[number, pl.ds(0, size), :], sems.at[number])
+        copy.start()
+        pieces.append((here, present, copy))
+    for number, (out, size, offset, place, entries) in enumerate(plan):
+        here, present, copy = pieces[number]
+        copy.wait()
+        rows = staged.at[number]
+        finish(rows, here, size)
         for n in range(out.shape[1] // TILE):
             cols = slice(n * TILE, (n + 1) * TILE)
-            value = spread(table, rows, here, size, present, n)
+            value = spread(table, rows, 0, size, present, n)
             out[:, cols] = value if entries is None else value + entries[:, cols]
 
 
-def assemble_kernel(place, table, leaf, sep, upd, *outs):
-    assemble(table, place[0], place[1], lambda here, size: (leaf, here), sep, upd, *outs)
+def assemble_kernel(place, table, leaf, sep, upd, *refs):
+    assemble(table, place[0], place[1], leaf, lambda rows, here, size: None, sep, upd, *refs)
 
 
 def assembled_shapes(sep, upd, level):
@@ -146,22 +155,22 @@
     return pl.pallas_call(
         assemble_kernel,
         out_shape=tuple(shapes),
-        in_specs=[SCALARS] * 2 + [WHOLE] * 3,
+        in_specs=[SCALARS] * 2 + [pl.BlockSpec(memory_space=pl.ANY)] + [WHOLE] * 2,
         out_specs=(WHOLE,) * 4,
+        scratch_shapes=[pltpu.VMEM((4, upd.shape[0], UPD), jnp.float32), pltpu.SemaphoreType.DMA((4,))],
         compiler_params=pltpu.CompilerParams(vmem_limit_bytes=32 * 2**20),
     )(place, table, leaf, sep, upd)
 
 
 def update_kernel(place, table, solved, rest, sep, upd, *refs):
-    outs, (high, low, child) = refs[:4], refs[4:]
+    outs, (staged, sems, high, low) = refs[:4], refs[4:]
     high[...], low[...] = split(solved[...])
 
-    def update_rows(here, size):
+    def finish(rows, here, size):
         left = split(solved[pl.ds(here, size), :])
-        child[:size, :] = rest[pl.ds(here, size), :] - dot3(left, (high[...], low[...]))
-        return child, 0
-
-    assemble(table, place[0], place[1], update_rows, sep, upd, *outs)
+        rows[:size, :] = rows[:size, :] - dot3(left, (high[...], low[...]))
+
+    assemble(table, place[0], place[1], rest, finish, sep, upd, *outs, staged, sems)
 
 
 def update(place, table, solved, rest, sep, upd, level):
@@ -169,12 +178,13 @@
     return pl.pallas_call(
         update_kernel,
         out_shape=tuple(shapes),
-        in_specs=[SCALARS] * 2 + [WHOLE] * 4,
+        in_specs=[SCALARS] * 2 + [WHOLE, pl.BlockSpec(memory_space=pl.ANY), WHOLE, WHOLE],
         out_specs=(WHOLE,) * 4,
         scratch_shapes=[
+            pltpu.VMEM((4, upd.shape[0], UPD), jnp.float32),
+            pltpu.SemaphoreType.DMA((4,)),
             pltpu.VMEM((UPD, SEP), jnp.bfloat16),
             pltpu.VMEM((UPD, SEP), jnp.bfloat16),
-            pltpu.VMEM((upd.shape[0], UPD), jnp.float32),
         ],
         compiler_params=pltpu.CompilerParams(vmem_limit_bytes=40 * 2**20),
     )(place, table, solved, rest, sep, upd)
@@ -260,11 +270,13 @@
 
     chains = []
     orders = orders_of(level, front_bits)
-    for item, buffer in enumerate(buffers):
-        for part, columns in enumerate(column_parts(buffer.shape[-1], len(orders))):
-            slot = item * len(orders) + part
-            chains.append(doubling(buffer, dims, orders[part], columns, all_send.at[slot], all_recv.at[slot]))
-    early, late = chains[:len(orders)], chains[len(orders):]
+    blocks = SEP // TILE
+    pieces = [(f11, (b * TILE, TILE), orders[b % len(orders)]) for b in range(blocks)]
+    for buffer in buffers[1:]:
+        pieces += [(buffer, columns, order) for columns, order in zip(column_parts(buffer.shape[-1], len(orders)), orders)]
+    for slot, (buffer, columns, order) in enumerate(pieces):
+        chains.append(doubling(buffer, dims, order, columns, all_send.at[slot], all_recv.at[slot]))
+    early, late = chains[:blocks], chains[blocks:]
     own = tuple(bits)
 
     def advance(which, step):
@@ -276,11 +288,14 @@
 
     sep_copy.wait()
     f11[own] = own_sep[...] + recv_sep[...]
-    advance(early, -1)
-    for step in range(steps):
-        if step == steps - 1:
-            upd_copy.start()
-        advance(early, step)
+    def skewed(turn):
+        for b in range(blocks):
+            if -1 <= turn - b < steps:
+                advance(early[b:b + 1], turn - b)
+
+    for turn in range(-1, steps):
+        skewed(turn)
+    upd_copy.start()
 
     def arrived():
         upd_copy.wait()
@@ -291,12 +306,16 @@
             f22[own] = own_upd[:, SEP:] + recv_upd[:, SEP:]
             advance(late, -1)
 
-    blocks = SEP // TILE
     flat = (slice(None),) * len(dims)
 
     @pl.loop(0, blocks)
     def _(b):
         pivot_block(b, lambda here: f11[flat + (slice(None), here)].reshape(SEP, TILE), full_diag, work, inv, high, low)
+
+        for done in range(blocks - 1):
+            @pl.when(b == done)
+            def _():
+                skewed(steps + done)
 
         @pl.when(b == 0)
         def _():
@@ -342,7 +361,7 @@
     scratch += [lead + (sep_count, SEP), (SEP, SEP), (SEP, TILE), (SEP // TILE, TILE, TILE)]
     halves = [(SEP, SEP)] * 2 + [(rows, SEP)] * 2
     received = [own_sep.shape, own_upd.shape]
-    chains = len(orders_of(level, front_bits)) * (1 if last else 3)
+    chains = SEP // TILE + len(orders_of(level, front_bits)) * (0 if last else 2)
     return pl.pallas_call(
         functools.partial(level_kernel, level, front_bits),
         out_shape=tuple(jax.ShapeDtypeStruct(shape, jnp.float32) for shape in shapes),

time: 198 us -> 207 us (1.045)
  Pallas kernels: 181 us -> 191 us
    pallas_call x3, Pallas kernels: 172 us -> 179 us  [factor_level(): pl.pallas_call(functools.partial(level_kernel, level, front_bits), out_sh...]
    pallas_call x2, Pallas kernels: 8.57 us -> 10.9 us  [update(): pl.pallas_call(update_kernel, out_shape=tuple(shapes), in_specs=[SCALARS]...]
where the time goes in v4:
time: 207 us; the launch traced here: 206 us
  Pallas kernels  191 us (92%)
  local copies, waits for them, and re-layouts  14 us (7%)
    pallas_call x3, Pallas kernels, factor_level(): pl.pallas_call(functools.partial(level_kernel, level, front_bits), out_sh...  179 us
    unnamed x26, local copies, waits for them, and re-layouts  12.6 us
    pallas_call x2, Pallas kernels, update(): pl.pallas_call(update_kernel, out_shape=tuple(shapes), in_specs=[SCALARS]...  10.9 us

profile of v4, /device:TPU:0, one launch (start us, length us, event | category | flops | bytes accessed | tf_op | source)
XLA Modules:
  0.0 206.3 jit_solution(17847089707053113854)
XLA Ops:
  0.6 0.0 copy-start
  0.6 0.0 copy-start.7
  0.7 0.1 pad_add_fusion
  0.8 0.1 pad_add_fusion.4.place
  0.9 0.7 fusion.5
  1.6 0.7 fusion.4
  2.3 0.0 copy-done
  2.3 0.1 fusion.2
  2.4 0.1 select_reduce_fusion.2
  2.5 0.1 fusion.1
  2.5 0.1 select_reduce_fusion.1
  2.6 0.1 pad_add_fusion.1
  2.7 0.1 fusion
  2.8 0.1 select_reduce_fusion
  2.9 0.1 pad_add_fusion.5.table
  3.0 0.0 copy-start.1
  3.0 2.2 %copy-done.1 = f32[1024,1024]{1,0:T(8,128)S(1)} copy-done((f32[1024,1024]{1,0:T(8,128)S(1)}, f32[1024,1024]{1,0:T(8,128)}, u32[]{:S(2)}) %copy-start.1) | copy-done | bytes 4194328
  5.2 0.0 copy-start.4
  5.2 1.1 copy-done.4
  6.3 0.0 copy-start.5
  6.3 1.0 copy-done.5
  7.3 0.0 copy-start.6
  7.3 1.0 shard_map.145
  8.3 0.0 copy-start.8
  8.3 0.0 copy-start.9
  8.3 72.3 %shard_map.146 = (f32[64,512]{1,0:T(8,128)S(1)}, f32[128,512]{1,0:T(8,128)S(1)}, f32[1024,512]{1,0:T(8,128)S(1)}, f32[2,2,2,128,1024]{4,3,2,1,0:T(8,128)}) custom-call(f32[64,512]{1,0:T(8,128)S(1)} %get-tuple-element.28.own_sep, f32[128,1536]{1,0:T(8,128)S(1)} %get-tuple-element.29.own_upd, f32[64,512]{1,0:T(8,128)S(1)} %get-tuple-element.30.out_sep, ...), custom_call_target="tpu_custom_call" | custom-call | tf_op jit(solution)/shard_map/pallas_call | solution.py:365
  80.6 0.0 copy-done.7
  80.6 0.0 copy-done.6
  80.7 0.0 copy-start.2
  80.7 2.2 %copy-done.2 = f32[2,2,2,128,1024]{4,3,2,1,0:T(8,128)S(1)} copy-done((f32[2,2,2,128,1024]{4,3,2,1,0:T(8,128)S(1)}, f32[2,2,2,128,1024]{4,3,2,1,0:T(8,128)}, u32[]{:S(2)}) %copy-start.2) | copy-done | bytes 4194328
  82.8 5.6 %shard_map.147 = (f32[32,512]{1,0:T(8,128)S(1)}, f32[64,1536]{1,0:T(8,128)S(1)}, f32[32,512]{1,0:T(8,128)S(1)}, f32[64,1536]{1,0:T(8,128)S(1)}) custom-call(s32[2]{0:T(128)S(1)} %get-tuple-element.51.place, s32[24]{0:T(128)S(1)} %get-tuple-element.53.table, f32[1024,512]{1,0:T(8,128)S(1)} %get-tuple-element.34.solved, f32[1024,1024]{1,0:T(8,128)S(1)} %bitcast.14, ...), custom_call_target="tpu_custom_call" | custom-call | tf_op jit(solution)/shard_map/pallas_call | solution.py:178
  88.4 59.4 %shard_map.148 = (f32[32,512]{1,0:T(8,128)S(1)}, f32[64,512]{1,0:T(8,128)S(1)}, f32[1024,512]{1,0:T(8,128)S(1)}, f32[2,2,2,2,64,1024]{5,4,3,2,1,0:T(8,128)}) custom-call(f32[32,512]{1,0:T(8,128)S(1)} %get-tuple-element.36.own_sep, f32[64,1536]{1,0:T(8,128)S(1)} %get-tuple-element.37.own_upd, f32[32,512]{1,0:T(8,128)S(1)} %get-tuple-element.38.out_sep, ...), custom_call_target="tpu_custom_call" | custom-call | tf_op jit(solution)/shard_map/pallas_call | solution.py:365
  147.8 0.0 copy-done.8
  147.9 0.0 copy-done.9
  147.9 0.0 copy-start.3
  147.9 2.2 %copy-done.3 = f32[2,2,2,2,64,1024]{5,4,3,2,1,0:T(8,128)S(1)} copy-done((f32[2,2,2,2,64,1024]{5,4,3,2,1,0:T(8,128)S(1)}, f32[2,2,2,2,64,1024]{5,4,3,2,1,0:T(8,128)}, u32[]{:S(2)}) %copy-start.3) | copy-done | bytes 4194328
  150.1 5.3 %shard_map.149 = (f32[16,512]{1,0:T(8,128)S(1)}, f32[32,512]{1,0:T(8,128)S(1)}, f32[16,512]{1,0:T(8,128)S(1)}, f32[32,512]{1,0:T(8,128)S(1)}) custom-call(s32[2]{0:T(128)S(1)} %pad_add_fusion.4.place, s32[24]{0:T(128)S(1)} %pad_add_fusion.5.table, f32[1024,512]{1,0:T(8,128)S(1)} %get-tuple-element.42.solved, f32[1024,1024]{1,0:T(8,128)S(1)} %bitcast.15, ...), custom_call_target="tpu_custom_call" | custom-call | tf_op jit(solution)/shard_map/pallas_call | solution.py:178
  155.4 47.0 %shard_map.150 = (f32[16,512]{1,0:T(8,128)S(1)}, f32[32,512]{1,0:T(8,128)S(1)}) custom-call(f32[16,512]{1,0:T(8,128)S(1)} %get-tuple-element.44.own_sep, f32[32,512]{1,0:T(8,128)S(1)} %get-tuple-element.45.own_upd, f32[16,512]{1,0:T(8,128)S(1)} %get-tuple-element.46.out_sep, f32[32,512]{1,0:T(8,128)S(1)} %get-tuple-element.47.out_upd), custom_call_target="tpu_custom_call" | custom-call | tf_op jit(solution)/shard_map/pallas_call | solution.py:365
  202.4 0.7 copy.22
  203.1 0.7 copy.23
  203.8 0.6 copy.24
  204.4 0.7 copy.25
  205.1 0.6 copy.26
  205.7 0.6 copy.27
  (4 shorter events, 0.0 us)
Async XLA Ops:
  0.6 1.6 copy-start
  0.6 80.0 %copy-start.7 = (f32[32,1536]{1,0:T(8,128)S(1)}, f32[32,1536]{1,0:T(8,128)}, u32[]{:S(2)}) copy-start(f32[32,1536]{1,0:T(8,128)} %sep.4) | copy-start | bytes 589828
  3.0 2.2 %copy-start.1 = (f32[1024,1024]{1,0:T(8,128)S(1)}, f32[1024,1024]{1,0:T(8,128)}, u32[]{:S(2)}) copy-start(f32[1024,1024]{1,0:T(8,128)} %leaf.1) | copy-start | bytes 12582916
  5.2 1.1 copy-start.4
  6.3 1.0 copy-start.5
  7.3 73.4 %copy-start.6 = (f32[64,1536]{1,0:T(8,128)S(1)}, f32[64,1536]{1,0:T(8,128)}, u32[]{:S(2)}) copy-start(f32[64,1536]{1,0:T(8,128)} %upd.4) | copy-start | bytes 1179652
  8.3 139.5 %copy-start.8 = (f32[32,1536]{1,0:T(8,128)S(1)}, f32[32,1536]{1,0:T(8,128)}, u32[]{:S(2)}) copy-start(f32[32,1536]{1,0:T(8,128)} %upd.5) | copy-start | bytes 589828
  8.3 139.5 %copy-start.9 = (f32[16,1536]{1,0:T(8,128)S(1)}, f32[16,1536]{1,0:T(8,128)}, u32[]{:S(2)}) copy-start(f32[16,1536]{1,0:T(8,128)} %sep.5) | copy-start | bytes 294916
  80.7 2.2 %copy-start.2 = (f32[2,2,2,128,1024]{4,3,2,1,0:T(8,128)S(1)}, f32[2,2,2,128,1024]{4,3,2,1,0:T(8,128)}, u32[]{:S(2)}) copy-start(f32[2,2,2,128,1024]{4,3,2,1,0:T(8,128)} %get-tuple-element.35) | copy-start | bytes 12582916
  147.9 2.2 %copy-start.3 = (f32[2,2,2,2,64,1024]{5,4,3,2,1,0:T(8,128)S(1)}, f32[2,2,2,2,64,1024]{5,4,3,2,1,0:T(8,128)}, u32[]{:S(2)}) copy-start(f32[2,2,2,2,64,1024]{5,4,3,2,1,0:T(8,128)} %get-tuple-element.43) | copy-start | bytes 12582916

commit v5 on v3

--- a/solution.py
+++ b/solution.py
@@ -253,6 +253,8 @@
     sep_copy = to_sibling(out_sep, recv_sep, 0)
     upd_copy = to_sibling(out_upd, recv_upd, 1)
     sep_copy.start()
+    if last:
+        upd_copy.start()
     high[...] = jnp.zeros_like(high)
     low[...] = jnp.zeros_like(low)
     done_high[...] = jnp.zeros_like(done_high)
@@ -261,7 +263,11 @@
     chains = []
     orders = orders_of(level, front_bits)
     for item, buffer in enumerate(buffers):
-        for part, columns in enumerate(column_parts(buffer.shape[-1], len(orders))):
+        parts = column_parts(buffer.shape[-1], len(orders))
+        if level == 1 and item > 0:
+            head = buffer.shape[-1] * 3 // 4
+            parts = [(0, head), (head, buffer.shape[-1] - head)]
+        for part, columns in enumerate(parts):
             slot = item * len(orders) + part
             chains.append(doubling(buffer, dims, orders[part], columns, all_send.at[slot], all_recv.at[slot]))
     early, late = chains[:len(orders)], chains[len(orders):]
@@ -278,7 +284,7 @@
     f11[own] = own_sep[...] + recv_sep[...]
     advance(early, -1)
     for step in range(steps):
-        if step == steps - 1:
+        if step == steps - 1 and not last:
             upd_copy.start()
         advance(early, step)
 
@@ -294,30 +300,43 @@
     blocks = SEP // TILE
     flat = (slice(None),) * len(dims)
 
-    @pl.loop(0, blocks)
-    def _(b):
+    def next_pivot(b):
         pivot_block(b, lambda here: f11[flat + (slice(None), here)].reshape(SEP, TILE), full_diag, work, inv, high, low)
 
-        @pl.when(b == 0)
-        def _():
-            arrived()
-
-        if not last:
-            for step in range(steps - 1):
-                @pl.when(b == blocks - steps + 1 + step)
-                def _():
-                    advance(late, step)
-
-    for chain in late[:len(orders)]:
-        chain[steps - 1].wait()
-
-    @pl.loop(0, blocks)
-    def _(b):
+    def next_solve(b):
         if last:
             piece = lambda here: below[:, here]
         else:
             piece = lambda here: f21[flat + (slice(None), here)].reshape(UPD, TILE)
         solve_block(b, piece, full_solved, inv, high, low, done_high, done_low)
+
+    if last:
+        arrived()
+
+        @pl.loop(0, blocks)
+        def _(b):
+            next_pivot(b)
+            next_solve(b)
+    else:
+        @pl.loop(0, blocks)
+        def _(b):
+            next_pivot(b)
+
+            @pl.when(b == 0)
+            def _():
+                arrived()
+
+            for step in range(steps - 1):
+                @pl.when(b == blocks - steps + 1 + step)
+                def _():
+                    advance(late, step)
+
+        for chain in late[:len(orders)]:
+            chain[steps - 1].wait()
+
+        @pl.loop(0, blocks)
+        def _(b):
+            next_solve(b)
 
     sep_count, upd_count = diag.shape[0], solved.shape[0]
     diag[...] = full_diag[pl.ds(pl.multiple_of(position * sep_count, 8), sep_count), :]

time: 198 us -> 210 us (1.061)
  Pallas kernels: 181 us -> 193 us
    pallas_call x3, Pallas kernels: 172 us -> 184 us  [factor_level(): pl.pallas_call(functools.partial(level_kernel, level, front_bits), out_sh...]
where the time goes in v5:
time: 210 us; the launch traced here: 209 us
  Pallas kernels  193 us (92%)
  local copies, waits for them, and re-layouts  14 us (7%)
    pallas_call x3, Pallas kernels, factor_level(): pl.pallas_call(functools.partial(level_kernel, level, front_bits), out_sh...  184 us
    unnamed x26, local copies, waits for them, and re-layouts  12.6 us
    pallas_call x2, Pallas kernels, update(): pl.pallas_call(update_kernel, out_shape=tuple(shapes), in_specs=[SCALARS]...  8.57 us

profile of v5, /device:TPU:0, one launch (start us, length us, event | category | flops | bytes accessed | tf_op | source)
XLA Modules:
  0.0 209.1 jit_solution(16935569060424983668)
XLA Ops:
  0.6 0.0 copy-start
  0.6 0.0 copy-start.7
  0.7 0.1 pad_add_fusion
  0.8 0.1 pad_add_fusion.4.place
  0.9 0.7 fusion.5
  1.6 0.7 fusion.4
  2.3 0.0 copy-done
  2.3 0.1 fusion.2
  2.4 0.1 select_reduce_fusion.2
  2.5 0.1 fusion.1
  2.5 0.1 select_reduce_fusion.1
  2.6 0.1 pad_add_fusion.1
  2.7 0.1 fusion
  2.8 0.1 select_reduce_fusion
  2.9 0.1 pad_add_fusion.5.table
  3.0 0.0 copy-start.1
  3.0 2.2 %copy-done.1 = f32[1024,1024]{1,0:T(8,128)S(1)} copy-done((f32[1024,1024]{1,0:T(8,128)S(1)}, f32[1024,1024]{1,0:T(8,128)}, u32[]{:S(2)}) %copy-start.1) | copy-done | bytes 4194328
  5.2 0.0 copy-start.4
  5.2 1.1 copy-done.4
  6.3 0.0 copy-start.5
  6.3 1.0 copy-done.5
  7.3 0.0 copy-start.6
  7.3 0.8 shard_map.145
  8.1 0.0 copy-start.8
  8.1 0.0 copy-start.9
  8.2 75.4 %shard_map.146 = (f32[64,512]{1,0:T(8,128)S(1)}, f32[128,512]{1,0:T(8,128)S(1)}, f32[1024,512]{1,0:T(8,128)S(1)}, f32[2,2,2,128,1024]{4,3,2,1,0:T(8,128)}) custom-call(f32[64,512]{1,0:T(8,128)S(1)} %get-tuple-element.28.own_sep, f32[128,1536]{1,0:T(8,128)S(1)} %get-tuple-element.29.own_upd, f32[64,512]{1,0:T(8,128)S(1)} %get-tuple-element.30.out_sep, ...), custom_call_target="tpu_custom_call" | custom-call | tf_op jit(solution)/shard_map/pallas_call | solution.py:365
  83.5 0.0 copy-done.7
  83.5 0.0 copy-done.6
  83.6 0.0 copy-start.2
  83.6 2.2 %copy-done.2 = f32[2,2,2,128,1024]{4,3,2,1,0:T(8,128)S(1)} copy-done((f32[2,2,2,128,1024]{4,3,2,1,0:T(8,128)S(1)}, f32[2,2,2,128,1024]{4,3,2,1,0:T(8,128)}, u32[]{:S(2)}) %copy-start.2) | copy-done | bytes 4194328
  85.7 4.5 %shard_map.147 = (f32[32,512]{1,0:T(8,128)S(1)}, f32[64,1536]{1,0:T(8,128)S(1)}, f32[32,512]{1,0:T(8,128)S(1)}, f32[64,1536]{1,0:T(8,128)S(1)}) custom-call(s32[2]{0:T(128)S(1)} %get-tuple-element.51.place, s32[24]{0:T(128)S(1)} %get-tuple-element.53.table, f32[1024,512]{1,0:T(8,128)S(1)} %get-tuple-element.34.solved, f32[1024,1024]{1,0:T(8,128)S(1)} %bitcast.14, ...), custom_call_target="tpu_custom_call" | custom-call | tf_op jit(solution)/shard_map/pallas_call | solution.py:169
  90.2 59.2 %shard_map.148 = (f32[32,512]{1,0:T(8,128)S(1)}, f32[64,512]{1,0:T(8,128)S(1)}, f32[1024,512]{1,0:T(8,128)S(1)}, f32[2,2,2,2,64,1024]{5,4,3,2,1,0:T(8,128)}) custom-call(f32[32,512]{1,0:T(8,128)S(1)} %get-tuple-element.36.own_sep, f32[64,1536]{1,0:T(8,128)S(1)} %get-tuple-element.37.own_upd, f32[32,512]{1,0:T(8,128)S(1)} %get-tuple-element.38.out_sep, ...), custom_call_target="tpu_custom_call" | custom-call | tf_op jit(solution)/shard_map/pallas_call | solution.py:365
  149.5 0.0 copy-done.8
  149.5 0.0 copy-done.9
  149.5 0.0 copy-start.3
  149.5 2.2 %copy-done.3 = f32[2,2,2,2,64,1024]{5,4,3,2,1,0:T(8,128)S(1)} copy-done((f32[2,2,2,2,64,1024]{5,4,3,2,1,0:T(8,128)S(1)}, f32[2,2,2,2,64,1024]{5,4,3,2,1,0:T(8,128)}, u32[]{:S(2)}) %copy-start.3) | copy-done | bytes 4194328
  151.7 4.1 %shard_map.149 = (f32[16,512]{1,0:T(8,128)S(1)}, f32[32,512]{1,0:T(8,128)S(1)}, f32[16,512]{1,0:T(8,128)S(1)}, f32[32,512]{1,0:T(8,128)S(1)}) custom-call(s32[2]{0:T(128)S(1)} %pad_add_fusion.4.place, s32[24]{0:T(128)S(1)} %pad_add_fusion.5.table, f32[1024,512]{1,0:T(8,128)S(1)} %get-tuple-element.42.solved, f32[1024,1024]{1,0:T(8,128)S(1)} %bitcast.15, ...), custom_call_target="tpu_custom_call" | custom-call | tf_op jit(solution)/shard_map/pallas_call | solution.py:169
  155.8 49.4 %shard_map.150 = (f32[16,512]{1,0:T(8,128)S(1)}, f32[32,512]{1,0:T(8,128)S(1)}) custom-call(f32[16,512]{1,0:T(8,128)S(1)} %get-tuple-element.44.own_sep, f32[32,512]{1,0:T(8,128)S(1)} %get-tuple-element.45.own_upd, f32[16,512]{1,0:T(8,128)S(1)} %get-tuple-element.46.out_sep, f32[32,512]{1,0:T(8,128)S(1)} %get-tuple-element.47.out_upd), custom_call_target="tpu_custom_call" | custom-call | tf_op jit(solution)/shard_map/pallas_call | solution.py:365
  205.2 0.7 copy.22
  205.9 0.7 copy.23
  206.6 0.6 copy.24
  207.2 0.7 copy.25
  207.9 0.6 copy.26
  208.5 0.6 copy.27
  (4 shorter events, 0.0 us)
Async XLA Ops:
  0.6 1.6 copy-start
  0.6 82.9 %copy-start.7 = (f32[32,1536]{1,0:T(8,128)S(1)}, f32[32,1536]{1,0:T(8,128)}, u32[]{:S(2)}) copy-start(f32[32,1536]{1,0:T(8,128)} %sep.4) | copy-start | bytes 589828
  3.0 2.2 %copy-start.1 = (f32[1024,1024]{1,0:T(8,128)S(1)}, f32[1024,1024]{1,0:T(8,128)}, u32[]{:S(2)}) copy-start(f32[1024,1024]{1,0:T(8,128)} %leaf.1) | copy-start | bytes 12582916
  5.2 1.1 copy-start.4
  6.3 1.0 copy-start.5
  7.3 76.3 %copy-start.6 = (f32[64,1536]{1,0:T(8,128)S(1)}, f32[64,1536]{1,0:T(8,128)}, u32[]{:S(2)}) copy-start(f32[64,1536]{1,0:T(8,128)} %upd.4) | copy-start | bytes 1179652
  8.1 141.3 %copy-start.8 = (f32[32,1536]{1,0:T(8,128)S(1)}, f32[32,1536]{1,0:T(8,128)}, u32[]{:S(2)}) copy-start(f32[32,1536]{1,0:T(8,128)} %upd.5) | copy-start | bytes 589828
  8.1 141.3 %copy-start.9 = (f32[16,1536]{1,0:T(8,128)S(1)}, f32[16,1536]{1,0:T(8,128)}, u32[]{:S(2)}) copy-start(f32[16,1536]{1,0:T(8,128)} %sep.5) | copy-start | bytes 294916
  83.6 2.2 %copy-start.2 = (f32[2,2,2,128,1024]{4,3,2,1,0:T(8,128)S(1)}, f32[2,2,2,128,1024]{4,3,2,1,0:T(8,128)}, u32[]{:S(2)}) copy-start(f32[2,2,2,128,1024]{4,3,2,1,0:T(8,128)} %get-tuple-element.35) | copy-start | bytes 12582916
  149.5 2.2 %copy-start.3 = (f32[2,2,2,2,64,1024]{5,4,3,2,1,0:T(8,128)S(1)}, f32[2,2,2,2,64,1024]{5,4,3,2,1,0:T(8,128)}, u32[]{:S(2)}) copy-start(f32[2,2,2,2,64,1024]{5,4,3,2,1,0:T(8,128)} %get-tuple-element.43) | copy-start | bytes 12582916
